TPU v7x, 32 devices: a whole 2x2x4 slice. The times are simulated.
32 devices in a mesh: shot: 2 (over core), space: 16 (over z, y, x).
Axes of the slice: x: 2, y: 2, z: 4, core: 2. Of those that a mesh axis runs over, the one named last changes fastest.
Arguments:
- medium_celerity: float32 [32, 32, 512], P('space'), may hold values from 1400 to 3000
- preceding_wave_snapshot: bfloat16 [4, 32, 32, 512], P('shot', 'space'), may hold values from -0.5 to 1.5
- entry_wave_snapshot: bfloat16 [4, 32, 32, 512], P('shot', 'space'), may hold values from -0.5 to 1.5
- costate_beyond_snapshot: bfloat16 [4, 32, 32, 512], P('shot', 'space'), may hold values from -6 to 6
- costate_terminal_snapshot: bfloat16 [4, 32, 32, 512], P('shot', 'space'), may hold values from -6 to 6
- signature_series: float32 [6], replicated, may hold values from -8 to 8
- emitter_indicator: int32 [4, 1024], P('shot'), may hold values 0 or 1
- probe_locations: int32 [3, 1024], replicated, may hold values from 0 to 511, as said below
- acquired_recordings: float32 [4, 6, 1024], P('shot'), may hold values from 0 to 2
Outputs:
- final_field: bfloat16 [4, 32, 32, 512], P('shot', 'space')
- amplitude: float32 [4], P('shot')
- gradient: float32 [32, 32, 512], P('space')
Inputs may be any that keep to these rules, and one draw needn't show every extreme that they name: probe_locations[0] is below 32, probe_locations[1] below 32, probe_locations[2] below 512; transducers may share a cell.
All inputs are finite; a program needn't handle non-finite values. No bound on the sum of `emitter_indicator` on one device may be relied on, other than what follows from the above.
Results may differ from a plain program's by a relative error of at most 0.033.
Values may be sent and summed in bfloat16 or wider, within the bound.
A program may use at most 576 MiB of HBM per device.

v0:
```python
import jax
import jax.numpy as jnp
from jax import lax
from jax.sharding import PartitionSpec as P

TICK_TALLY = 6


SPEED_SCALE = 1.0 / 6000.0
EPSILON = 1e-06


def extended(array, sides, width):
    for axis, dim in sides:
        peers, length = (lax.axis_size(axis), array.shape[dim])
        up = [(i, (i + 1) % peers) for i in range(peers - 1)]
        down = [(j, i) for i, j in up]
        last = lax.slice_in_dim(array, length - width, length, axis=dim)
        initial = lax.slice_in_dim(array, 0, width, axis=dim)
        before = lax.ppermute(last, axis, up)
        after = lax.ppermute(initial, axis, down)
        array = jnp.concatenate([before, array, after], axis=dim)
    return array


def laplace_rim(center):
    middle = center[:, 1:-1]
    padded = jnp.pad(middle, ((0, 0), (0, 0), (1, 1), (1, 1)))
    return (
        center[:, 2:]
        + center[:, :-2]
        + padded[:, :, 2:, 1:-1]
        + padded[:, :, :-2, 1:-1]
        + padded[:, :, 1:-1, 2:]
        + padded[:, :, 1:-1, :-2]
        - 6.0 * middle
    )


def add_sources(field, values, target):
    shape = field.shape
    flat_field = field.reshape(shape[0], -1).at[:, target].add(values, mode="drop")
    return flat_field.reshape(shape)


def step_field(earlier, center, courant, values, target):
    center_f = center.astype(jnp.float32)
    following = (
        2.0 * center_f[:, 1:-1] - earlier.astype(jnp.float32) + courant * laplace_rim(center_f)
    )
    return add_sources(following, values, target)


def body(
    medium_celerity,
    preceding_wave_snapshot,
    entry_wave_snapshot,
    costate_beyond_snapshot,
    costate_terminal_snapshot,
    signature_series,
    emitter_indicator,
    probe_locations,
    acquired_recordings,
):
    planes = medium_celerity.shape[0]
    row_count = medium_celerity.shape[1]
    col_count = medium_celerity.shape[2]
    shot_count = entry_wave_snapshot.shape[0]
    cell_count = planes * row_count * col_count
    lowest = lax.axis_index("space") * planes
    courant = (medium_celerity * SPEED_SCALE) ** 2
    local_plane = probe_locations[0] - lowest
    shifted = local_plane + 0
    inside = (shifted >= 0) & (shifted < planes + 2 * 0)
    flat_index = (shifted * row_count + probe_locations[1]) * col_count + probe_locations[2]
    outside_index = (planes + 2 * 0) * row_count * col_count
    target_zero = jnp.where(inside, flat_index, outside_index)
    picked = jnp.clip(target_zero, 0, cell_count - 1)
    ownership = inside.astype(jnp.float32)

    def sample(field):
        return (
            jnp.take(field.reshape(shot_count, -1), picked, axis=1).astype(jnp.float32) * ownership
        )

    def march(first_field, second_field, injections):
        produced = []
        earlier, current = (first_field, second_field)
        for step_index in range(len(injections)):
            center = extended(current, (("space", 1),), 1)
            following = step_field(
                earlier, center, courant, injections[step_index], target_zero
            ).astype(jnp.bfloat16)
            produced.append(following)
            earlier, current = (current, following)
        return produced

    inject_signal = emitter_indicator.astype(jnp.float32)
    sources = [inject_signal * signature_series[step_index] for step_index in range(TICK_TALLY)]
    forward = march(preceding_wave_snapshot, entry_wave_snapshot, sources)
    local_traces = jnp.stack([sample(field) for field in forward], axis=1)
    synthetic = lax.psum(local_traces, "space")
    amplitude = jnp.sum(acquired_recordings * synthetic, axis=(1, 2)) / (
        jnp.sum(synthetic * synthetic, axis=(1, 2)) + EPSILON
    )
    misfit = amplitude[:, None, None] * synthetic - acquired_recordings
    adjoint_sources = [
        misfit[:, TICK_TALLY - 1 - step_index, :] for step_index in range(TICK_TALLY)
    ]
    backward = march(costate_beyond_snapshot, costate_terminal_snapshot, adjoint_sources)
    history = [preceding_wave_snapshot, entry_wave_snapshot] + forward
    total = jnp.zeros((planes, row_count, col_count), jnp.float32)
    for step_index in range(TICK_TALLY):
        moment = TICK_TALLY - 1 - step_index
        curvature = (
            history[moment + 2].astype(jnp.float32)
            - 2.0 * history[moment + 1].astype(jnp.float32)
            + history[moment].astype(jnp.float32)
        )
        total = total + jnp.sum(backward[step_index].astype(jnp.float32) * curvature, axis=0)
    total = lax.psum(total.astype(jnp.bfloat16), "shot").astype(jnp.float32)
    weight = 2.0 * (1500.0 / medium_celerity) ** 3
    return (forward[-1], amplitude, weight * total)


def solution(mesh):
    placed = (
        P("space", None, None),
        P("shot", "space", None, None),
        P("shot", "space", None, None),
        P("shot", "space", None, None),
        P("shot", "space", None, None),
        P(),
        P("shot", None),
        P(),
        P("shot", None, None),
    )
    return jax.shard_map(
        body,
        mesh=mesh,
        in_specs=placed,
        out_specs=(P("shot", "space", None, None), P("shot"), P("space", None, None)),
        check_vma=False,
    )
```

profile of v0, /device:TPU:0, one launch (start us, length us, event | category | flops | bytes accessed | tf_op | source)
XLA Modules:
  0.0 828.1 jit_solution(10018884744188923097)
XLA Ops:
  33.0 8.6 %copy.134 = f32[2,2,32,512]{0,3,2,1:T(8,128)} copy(f32[2,2,32,512]{3,2,1,0:T(8,128)S(1)} %fusion.10) | data formatting | bytes 524288 | tf_op jit(solution)/shard_map/add | solution.py:49
  41.6 16.9 %scatter_fusion = f32[2,32768]{0,1:T(8,128)} fusion(f32[2,32768]{0,1:T(8,128)} %bitcast.97, s32[1024]{0:T(1024)S(1)} %bitcast.120, f32[1024,2]{1,0:T(8,128)S(1)} %copy.135), kind=kCustom, calls=%fused_computation.6 | custom fusion | flops 2048 | bytes 28672 | tf_op jit(solution)/shard_map/scatter-add | solution.py:42
  58.5 9.1 %convert_element_type.276 = bf16[2,32768]{0,1:T(8,128)(2,1)} convert(f32[2,32768]{0,1:T(8,128)} %scatter_fusion) | non-fusion elementwise | flops 65536 | bytes 393216 | tf_op jit(solution)/shard_map/convert_element_type | solution.py:93
  92.5 16.9 %scatter_fusion.1 = f32[2,32768]{0,1:T(8,128)} fusion(f32[2,32768]{0,1:T(8,128)} %bitcast.98, s32[1024]{0:T(1024)S(1)} %bitcast.121, f32[1024,2]{1,0:T(8,128)S(1)} %copy.140), kind=kCustom, calls=%fused_computation.7 | custom fusion | flops 2048 | bytes 28672 | tf_op jit(solution)/shard_map/scatter-add | solution.py:42
  109.4 8.9 %convert_element_type.280 = bf16[2,32768]{0,1:T(8,128)(2,1)} convert(f32[2,32768]{0,1:T(8,128)} %scatter_fusion.1) | non-fusion elementwise | flops 65536 | bytes 393216 | tf_op jit(solution)/shard_map/convert_element_type | solution.py:93
  142.9 16.9 %scatter_fusion.2 = f32[2,32768]{0,1:T(8,128)} fusion(f32[2,32768]{0,1:T(8,128)} %bitcast.99, s32[1024]{0:T(1024)S(1)} %bitcast.122, f32[1024,2]{1,0:T(8,128)S(1)} %copy.146), kind=kCustom, calls=%fused_computation.8 | custom fusion | flops 2048 | bytes 28672 | tf_op jit(solution)/shard_map/scatter-add | solution.py:42
  159.8 8.9 %convert_element_type.284 = bf16[2,32768]{0,1:T(8,128)(2,1)} convert(f32[2,32768]{0,1:T(8,128)} %scatter_fusion.2) | non-fusion elementwise | flops 65536 | bytes 393216 | tf_op jit(solution)/shard_map/convert_element_type | solution.py:93
  193.5 17.0 %scatter_fusion.3 = f32[2,32768]{0,1:T(8,128)} fusion(f32[2,32768]{0,1:T(8,128)} %bitcast.100, s32[1024]{0:T(1024)S(1)} %bitcast.123, f32[1024,2]{1,0:T(8,128)S(1)} %copy.152), kind=kCustom, calls=%fused_computation.9 | custom fusion | flops 2048 | bytes 28672 | tf_op jit(solution)/shard_map/scatter-add | solution.py:42
  210.4 8.8 %convert_element_type.288 = bf16[2,32768]{0,1:T(8,128)(2,1)} convert(f32[2,32768]{0,1:T(8,128)} %scatter_fusion.3) | non-fusion elementwise | flops 65536 | bytes 393216 | tf_op jit(solution)/shard_map/convert_element_type | solution.py:93
  244.2 17.0 %scatter_fusion.4 = f32[2,32768]{0,1:T(8,128)} fusion(f32[2,32768]{0,1:T(8,128)} %bitcast.101, s32[1024]{0:T(1024)S(1)} %bitcast.124, f32[1024,2]{1,0:T(8,128)S(1)} %copy.158), kind=kCustom, calls=%fused_computation.10 | custom fusion | flops 2048 | bytes 28672 | tf_op jit(solution)/shard_map/scatter-add | solution.py:42
  261.2 8.9 %convert_element_type.292 = bf16[2,32768]{0,1:T(8,128)(2,1)} convert(f32[2,32768]{0,1:T(8,128)} %scatter_fusion.4) | non-fusion elementwise | flops 65536 | bytes 393216 | tf_op jit(solution)/shard_map/convert_element_type | solution.py:93
  302.0 8.6 %copy.171 = f32[2,2,32,512]{0,3,2,1:T(8,128)} copy(f32[2,2,32,512]{3,2,1,0:T(8,128)S(1)} %get-tuple-element.34) | data formatting | bytes 524288 | tf_op jit(solution)/shard_map/add | solution.py:49
  344.9 17.0 %scatter_fusion.5 = f32[2,32768]{0,1:T(8,128)} fusion(f32[2,32768]{0,1:T(8,128)} %bitcast.102, s32[1024]{0:T(1024)S(1)} %bitcast.125, f32[1024,2]{1,0:T(8,128)S(1)} %copy.164), kind=kCustom, calls=%fused_computation.11 | custom fusion | flops 2048 | bytes 28672 | tf_op jit(solution)/shard_map/scatter-add | solution.py:42
  362.0 8.9 %convert_element_type.296 = bf16[2,32768]{0,1:T(8,128)(2,1)} convert(f32[2,32768]{0,1:T(8,128)} %scatter_fusion.5) | non-fusion elementwise | flops 65536 | bytes 393216 | tf_op jit(solution)/shard_map/convert_element_type | solution.py:93
  382.3 82.8 %psum.14 = f32[2,6,1024]{2,0,1:T(2,128)S(1)} all-reduce(f32[2,6,1024]{2,0,1:T(2,128)S(1)} %constant_dynamic-update-slice_fusion), channel_id=1, replica_groups=mesh['shot'=2,'space'=16] {'space'}, use_global_device_ids=true, to_apply=%region_6.8 | all-reduce | flops 12288 | bytes 98304 | tf_op jit(solution)/shard_map/psum | solution.py:102
  465.7 16.9 %scatter_fusion.6 = f32[2,32768]{0,1:T(8,128)} fusion(f32[2,32768]{0,1:T(8,128)} %bitcast.96, s32[1024]{0:T(1024)S(1)} %bitcast.126, f32[1024,2]{1,0:T(8,128)S(1)} %copy.172), kind=kCustom, calls=%fused_computation.12 | custom fusion | flops 2048 | bytes 28672 | tf_op jit(solution)/shard_map/scatter-add | solution.py:42
  482.6 8.9 %convert_element_type.306 = bf16[2,32768]{0,1:T(8,128)(2,1)} convert(f32[2,32768]{0,1:T(8,128)} %scatter_fusion.6) | non-fusion elementwise | flops 65536 | bytes 393216 | tf_op jit(solution)/shard_map/convert_element_type | solution.py:93
  515.2 16.9 %scatter_fusion.7 = f32[2,32768]{0,1:T(8,128)} fusion(f32[2,32768]{0,1:T(8,128)} %bitcast.103, s32[1024]{0:T(1024)S(1)} %bitcast.127, f32[1024,2]{1,0:T(8,128)S(1)} %copy.177), kind=kCustom, calls=%fused_computation.13 | custom fusion | flops 2048 | bytes 28672 | tf_op jit(solution)/shard_map/scatter-add | solution.py:42
  532.0 8.9 %convert_element_type.314 = bf16[2,32768]{0,1:T(8,128)(2,1)} convert(f32[2,32768]{0,1:T(8,128)} %scatter_fusion.7) | non-fusion elementwise | flops 65536 | bytes 393216 | tf_op jit(solution)/shard_map/convert_element_type | solution.py:93
  556.4 8.6 %copy.182 = f32[2,2,32,512]{0,3,2,1:T(8,128)} copy(f32[2,2,32,512]{3,2,1,0:T(8,128)S(1)} %fusion.76) | data formatting | bytes 524288 | tf_op jit(solution)/shard_map/add | solution.py:49
  565.0 16.9 %scatter_fusion.8 = f32[2,32768]{0,1:T(8,128)} fusion(f32[2,32768]{0,1:T(8,128)} %bitcast.104, s32[1024]{0:T(1024)S(1)} %bitcast.128, f32[1024,2]{1,0:T(8,128)S(1)} %copy.183), kind=kCustom, calls=%fused_computation.14 | custom fusion | flops 2048 | bytes 28672 | tf_op jit(solution)/shard_map/scatter-add | solution.py:42
  581.9 8.9 %convert_element_type.320 = bf16[2,32768]{0,1:T(8,128)(2,1)} convert(f32[2,32768]{0,1:T(8,128)} %scatter_fusion.8) | non-fusion elementwise | flops 65536 | bytes 393216 | tf_op jit(solution)/shard_map/convert_element_type | solution.py:93
  606.8 8.6 %copy.188 = f32[2,2,32,512]{0,3,2,1:T(8,128)} copy(f32[2,2,32,512]{3,2,1,0:T(8,128)S(1)} %fusion.83) | data formatting | bytes 524288 | tf_op jit(solution)/shard_map/add | solution.py:49
  615.4 16.9 %scatter_fusion.9 = f32[2,32768]{0,1:T(8,128)} fusion(f32[2,32768]{0,1:T(8,128)} %bitcast.107, s32[1024]{0:T(1024)S(1)} %bitcast.129, f32[1024,2]{1,0:T(8,128)S(1)} %copy.189), kind=kCustom, calls=%fused_computation.15 | custom fusion | flops 2048 | bytes 28672 | tf_op jit(solution)/shard_map/scatter-add | solution.py:42
  632.3 54.8 %fusion.6 = (f32[32768]{0:T(1024)S(1)}, f32[32768]{0:T(1024)S(1)}, f32[32768]{0:T(1024)S(1)}, f32[32768]{0:T(1024)S(1)}, bf16[2,32768]{0,1:T(8,128)(2,1)}) fusion(f32[2,32768]{0,1:T(8,128)} %scatter_fusion.9, f32[2,32768]{0,1:T(8,128)} %scatter_fusion.8, f32[2,32768]{0,1:T(8,128)} %scatter_fusion.7, f32[2,32768]{0,1:T(8,128)} %scatter_fusion.6, ...), kind=kLoop, calls=%fused_computation.34 | loop fusion | flops 2490368 | bytes 3276800 | tf_op jit(solution)/shard_map/reduce_sum | solution.py:120
  703.5 8.6 %copy.194 = f32[2,2,32,512]{0,3,2,1:T(8,128)} copy(f32[2,2,32,512]{3,2,1,0:T(8,128)S(1)} %fusion.90) | data formatting | bytes 524288 | tf_op jit(solution)/shard_map/add | solution.py:49
  712.1 16.9 %scatter_fusion.10 = f32[2,32768]{0,1:T(8,128)} fusion(f32[2,32768]{0,1:T(8,128)} %bitcast.106, s32[1024]{0:T(1024)S(1)} %bitcast.130, f32[1024,2]{1,0:T(8,128)S(1)} %copy.195), kind=kCustom, calls=%fused_computation.16 | custom fusion | flops 2048 | bytes 28672 | tf_op jit(solution)/shard_map/scatter-add | solution.py:42
  729.0 8.9 %convert_element_type.332 = bf16[2,32768]{0,1:T(8,128)(2,1)} convert(f32[2,32768]{0,1:T(8,128)} %scatter_fusion.10) | non-fusion elementwise | flops 65536 | bytes 393216 | tf_op jit(solution)/shard_map/convert_element_type | solution.py:93
  754.2 8.6 %copy.201 = f32[2,2,32,512]{0,3,2,1:T(8,128)} copy(f32[2,2,32,512]{3,2,1,0:T(8,128)S(1)} %fusion.97) | data formatting | bytes 524288 | tf_op jit(solution)/shard_map/add | solution.py:49
  762.9 16.9 %scatter_fusion.11 = f32[2,32768]{0,1:T(8,128)} fusion(f32[2,32768]{0,1:T(8,128)} %bitcast.105, s32[1024]{0:T(1024)S(1)} %bitcast.131, f32[1024,2]{1,0:T(8,128)S(1)} %copy.202), kind=kCustom, calls=%fused_computation.17 | custom fusion | flops 2048 | bytes 28672 | tf_op jit(solution)/shard_map/scatter-add | solution.py:42
  779.8 9.2 %convert_element_type.337 = bf16[2,32768]{0,1:T(8,128)(2,1)} convert(f32[2,32768]{0,1:T(8,128)} %scatter_fusion.11) | non-fusion elementwise | flops 65536 | bytes 393216 | tf_op jit(solution)/shard_map/convert_element_type | solution.py:93
  804.7 14.6 %all-reduce.14.cloned.1.call-done = bf16[2,32,512]{2,1,0:T(8,128)(2,1)} async-done(((bf16[2,32,512]{2,1,0:T(8,128)(2,1)}), bf16[2,32,512]{2,1,0:T(8,128)(2,1)}) %all-reduce.14.cloned.1.call-update) | async-done | bytes 65552 | tf_op jit(solution)/shard_map/psum | solution.py:121
  (187 shorter events, 307.5 us)
Async XLA Ops:
  7.2 812.1 %all-reduce.14.cloned.1.call-start = ((), (), s32[]{:S(2)}) async-start(), calls=%async_computation | async-start | bytes 131072 | tf_op jit(solution)/shard_map/psum | solution.py:121
  8.1 73.3 %collective-permute-start.13 = (bf16[2,1,32,512]{3,2,1,0:T(8,128)(2,1)S(1)}, bf16[2,1,32,512]{3,2,1,0:T(8,128)(2,1)S(1)}, u32[]{:S(2)}, u32[]{:S(2)}) collective-permute-start(bf16[2,1,32,512]{3,2,1,0:T(8,128)(2,1)S(1)} %get-tuple-element.37), channel_id=1, source_target_pairs={{1,0},{2,1},{3,2},{4,3},{5,4},{6,5},{7,6},{8,7},{9,8},{10,9},{11,1... | collective-permute-start | bytes 196616 | tf_op jit(solution)/shard_map/ppermute | solution.py:21
  9.4 72.0 %collective-permute-start.12 = (bf16[2,1,32,512]{3,2,1,0:T(8,128)(2,1)S(1)}, bf16[2,1,32,512]{3,2,1,0:T(8,128)(2,1)S(1)}, u32[]{:S(2)}, u32[]{:S(2)}) collective-permute-start(bf16[2,1,32,512]{3,2,1,0:T(8,128)(2,1)S(1)} %get-tuple-element.36), channel_id=1, source_target_pairs={{0,1},{1,2},{2,3},{3,4},{4,5},{5,6},{6,7},{7,8},{8,9},{9,10},{10,1... | collective-permute-start | bytes 196616 | tf_op jit(solution)/shard_map/ppermute | solution.py:20
  15.8 15.1 %collective-permute-start.1 = (bf16[2,1,32,512]{3,2,1,0:T(8,128)(2,1)S(1)}, bf16[2,1,32,512]{3,2,1,0:T(8,128)(2,1)S(1)}, u32[]{:S(2)}, u32[]{:S(2)}) collective-permute-start(bf16[2,1,32,512]{3,2,1,0:T(8,128)(2,1)S(1)} %get-tuple-element.49), channel_id=1, source_target_pairs={{1,0},{2,1},{3,2},{4,3},{5,4},{6,5},{7,6},{8,7},{9,8},{10,9},{11,1... | collective-permute-start | bytes 196616 | tf_op jit(solution)/shard_map/ppermute | solution.py:21
  17.1 13.8 %collective-permute-start = (bf16[2,1,32,512]{3,2,1,0:T(8,128)(2,1)S(1)}, bf16[2,1,32,512]{3,2,1,0:T(8,128)(2,1)S(1)}, u32[]{:S(2)}, u32[]{:S(2)}) collective-permute-start(bf16[2,1,32,512]{3,2,1,0:T(8,128)(2,1)S(1)} %get-tuple-element.48), channel_id=1, source_target_pairs={{0,1},{1,2},{2,3},{3,4},{4,5},{5,6},{6,7},{7,8},{8,9},{9,10},{10,1... | collective-permute-start | bytes 196616 | tf_op jit(solution)/shard_map/ppermute | solution.py:20
  58.5 24.9 %copy-start.4 = (bf16[2,2,32,512]{3,2,1,0:T(8,128)(2,1)S(1)}, bf16[2,2,32,512]{3,2,1,0:T(8,128)(2,1)}, u32[]{:S(2)}) copy-start(bf16[2,2,32,512]{3,2,1,0:T(8,128)(2,1)} %param.13) | copy-start | bytes 393220
  58.5 24.9 %copy-start.10 = (bf16[2,2,32,512]{3,2,1,0:T(8,128)(2,1)S(1)}, bf16[2,2,32,512]{3,2,1,0:T(8,128)(2,1)}, u32[]{:S(2)}) copy-start(bf16[2,2,32,512]{3,2,1,0:T(8,128)(2,1)} %param.14) | copy-start | bytes 393220
  74.6 59.5 %copy-start = (bf16[2,2,32,512]{3,2,1,0:T(8,128)(2,1)}, bf16[2,2,32,512]{3,2,1,0:T(8,128)(2,1)S(1)}, u32[]{:S(2)}) copy-start(bf16[2,2,32,512]{3,2,1,0:T(8,128)(2,1)S(1)} %copy.136) | copy-start | bytes 393220
  74.7 7.1 collective-permute-start.3
  76.0 7.4 collective-permute-start.2
  125.3 59.4 %copy-start.2 = (bf16[2,2,32,512]{3,2,1,0:T(8,128)(2,1)}, bf16[2,2,32,512]{3,2,1,0:T(8,128)(2,1)S(1)}, u32[]{:S(2)}) copy-start(bf16[2,2,32,512]{3,2,1,0:T(8,128)(2,1)S(1)} %copy.141) | copy-start | bytes 393220
  125.3 7.0 collective-permute-start.5
  126.6 7.4 collective-permute-start.4
  175.7 8.1 collective-permute-start.7
  177.0 7.5 collective-permute-start.6
  226.3 8.0 collective-permute-start.9
  227.6 7.7 collective-permute-start.8
  277.2 58.9 %collective-permute-start.11 = (bf16[2,1,32,512]{3,2,1,0:T(8,128)(2,1)S(1)}, bf16[2,1,32,512]{3,2,1,0:T(8,128)(2,1)S(1)}, u32[]{:S(2)}, u32[]{:S(2)}) collective-permute-start(bf16[2,1,32,512]{3,2,1,0:T(8,128)(2,1)S(1)} %get-tuple-element.39), channel_id=1, source_target_pairs={{1,0},{2,1},{3,2},{4,3},{5,4},{6,5},{7,6},{8,7},{9,8},{10,9},{11,1... | collective-permute-start | bytes 196616 | tf_op jit(solution)/shard_map/ppermute | solution.py:21
  278.5 57.6 %collective-permute-start.10 = (bf16[2,1,32,512]{3,2,1,0:T(8,128)(2,1)S(1)}, bf16[2,1,32,512]{3,2,1,0:T(8,128)(2,1)S(1)}, u32[]{:S(2)}, u32[]{:S(2)}) collective-permute-start(bf16[2,1,32,512]{3,2,1,0:T(8,128)(2,1)S(1)} %get-tuple-element.38), channel_id=1, source_target_pairs={{0,1},{1,2},{2,3},{3,4},{4,5},{5,6},{6,7},{7,8},{8,9},{9,10},{10,1... | collective-permute-start | bytes 196616 | tf_op jit(solution)/shard_map/ppermute | solution.py:20
  344.9 120.3 %copy-start.9 = (f32[2,6,1024]{2,0,1:T(2,128)S(1)}, f32[2,6,1024]{2,0,1:T(2,128)}, u32[]{:S(2)}) copy-start(f32[2,6,1024]{2,0,1:T(2,128)} %param.19) | copy-start | bytes 147460
  465.4 33.2 %copy-start.11 = (f32[2]{0:T(128)}, f32[2]{0:T(128)S(1)}, u32[]{:S(2)}) copy-start(f32[2]{0:T(128)S(1)} %add_divide_fusion) | copy-start | bytes 28
  498.6 6.2 collective-permute-start.15
  499.9 6.4 collective-permute-start.14
  548.0 6.6 collective-permute-start.17
  549.3 6.8 collective-permute-start.16
  597.8 7.1 collective-permute-start.19
  599.1 7.3 collective-permute-start.18
  694.2 7.8 collective-permute-start.21
  695.5 7.7 collective-permute-start.20
  744.9 7.4 collective-permute-start.23
  746.2 7.7 collective-permute-start.22
  779.8 39.5 %copy-start.8 = (f32[2,32,512]{2,1,0:T(8,128)S(1)}, f32[2,32,512]{2,1,0:T(8,128)}, u32[]{:S(2)}) copy-start(f32[2,32,512]{2,1,0:T(8,128)} %param.11) | copy-start | bytes 393220
  (5 other events, 87.8 us)
Sparse Core Ops, SparseCore 0:
  796.9 22.3 all-reduce.13
where the time goes:
time: 840 us; the launch traced here: 828 us
  other arithmetic  373 us (44%)
  local copies, waits for them, and re-layouts  247 us (29%)
  blocking collectives  82.8 us (10%)
  starting transfers between devices  82.2 us (10%)
  waiting for transfers between devices  28.3 us (3%)
  between operations  15.4 us (2%)
    scatter-add x12, other arithmetic, add_sources(): field.reshape(shape[0], -1).at[:, target].add(values, mode='drop')  203 us
    add x12, local copies, waits for them, and re-layouts, step_field(): 2.0 * center_f[:, 1:-1] - earlier.astype(jnp.float32)  103 us
    convert_element_type x11, other arithmetic, march(): following = step_field(earlier, center, courant, injections[step_index],...  98.3 us
    psum x1, blocking collectives, body(): synthetic = lax.psum(local_traces, 'space')  82.8 us
    convert_element_type x10, local copies, waits for them, and re-layouts, march(): following = step_field(earlier, center, courant, injections[step_index],...  70.2 us
    ppermute x12, starting transfers between devices, extended(): before = lax.ppermute(last, axis, up)  66.6 us
    reduce_sum x2, other arithmetic, body(): jnp.sum(backward[step_index].astype(jnp.float32) * curvature, axis=0)  54.9 us
    gather x6, local copies, waits for them, and re-layouts, sample(): jnp.take(field.reshape(shot_count, -1), picked, axis=1).astype(jnp.float32)  51 us
  transfers between devices with their start and end apart: 25, of which 16 were waited for; matrix products, arithmetic and copies ran while one was open for 14% of the time, Pallas kernels for 0%

commit v1 on v0

v1 whole, which is shorter than its diff:
```python
import functools

import jax
import jax.numpy as jnp
from jax import lax
from jax.experimental import pallas as pl
from jax.experimental.pallas import tpu as pltpu
from jax.sharding import PartitionSpec as P

SPEED_SCALE = 1.0 / 6000.0
EPSILON = 1e-06
MESH = pl.DeviceIdType.MESH
F32 = jnp.float32
BF16 = jnp.bfloat16


def kernel(
    peers,
    velocity,
    preceding,
    entry,
    beyond,
    terminal,
    signature,
    emitters,
    locations,
    recordings,
    final,
    amplitude,
    gradient,
    forward,
    backward,
    forward_halo,
    backward_halo,
    courant,
    partial,
    column_hot,
    tally,
    fired,
    recorded,
    sums,
    products,
    gathered,
    total,
    outgoing,
    incoming,
    forward_sent,
    forward_got,
    backward_sent,
    backward_got,
    sums_sent,
    sums_got,
    total_sent,
    total_got,
):
    me = lax.axis_index("space")
    core = lax.axis_index("shot")
    shots, planes, rows, cols = entry.shape
    ticks = recordings.shape[1]
    last = planes - 1
    shot_range, plane_range = range(shots), range(planes)

    barrier = pltpu.get_barrier_semaphore()
    for d in range(1, peers):
        pl.semaphore_signal(
            barrier, inc=1, device_id={"space": lax.rem(me + d, peers)}, device_id_type=MESH
        )
    pl.semaphore_signal(barrier, inc=1, device_id={"shot": 1 - core}, device_id_type=MESH)
    pl.semaphore_wait(barrier, peers)

    def hop(field, halo, sent, got, side, j):
        return pltpu.make_async_remote_copy(
            src_ref=field.at[:, last if side == 0 else 0],
            dst_ref=halo.at[side, j],
            send_sem=sent.at[side, j],
            recv_sem=got.at[side, j],
            device_id={"space": me + 1 if side == 0 else me - 1},
            device_id_type=MESH,
        )

    def has_target(side):
        return me < peers - 1 if side == 0 else me > 0

    def has_source(side):
        return me > 0 if side == 0 else me < peers - 1

    def send(side, *args):
        @pl.when(has_target(side))
        def _():
            hop(*args[:4], side, args[4]).start()

    def receive(side, *args):
        @pl.when(has_source(side))
        def _():
            hop(*args[:4], side, args[4]).wait_recv()

    def drain(side, *args):
        @pl.when(has_target(side))
        def _():
            hop(*args[:4], side, args[4]).wait_send()

    ahead = [preceding, entry] + [forward.at[j] for j in range(ticks - 1)] + [final]
    back = [beyond, terminal] + [backward.at[j] for j in range(ticks)]
    ahead_link = (forward_halo, forward_sent, forward_got)
    back_link = (backward_halo, backward_sent, backward_got)

    for side in (1, 0):
        send(side, entry, *ahead_link, 0)
    for side in (1, 0):
        send(side, terminal, *back_link, 0)

    for side, here in ((0, me == 0), (1, me == peers - 1)):

        @pl.when(here)
        def _(side=side):
            forward_halo[side] = jnp.zeros_like(forward_halo[side])
            backward_halo[side] = jnp.zeros_like(backward_halo[side])

    courant[...] = (velocity[...] * SPEED_SCALE) ** 2

    probes = locations.shape[1]
    row_of = (locations[0:1, :] - me * planes) * rows + locations[1:2, :]
    row_hot = lax.broadcasted_iota(jnp.int32, (planes * rows, probes), 0) == row_of
    column_hot[...] = jnp.where(
        lax.broadcasted_iota(jnp.int32, (cols, probes), 0) == locations[2:3, :], 1.0, 0.0
    ).astype(BF16)

    def spread(left):
        return lax.dot_general(
            left, column_hot[...], (((1,), (1,)), ((), ())), preferred_element_type=F32
        )

    cells = planes * rows
    firing = emitters[...].astype(F32)
    lefts = [jnp.where(row_hot, 1.0, 0.0)]
    lefts += [jnp.where(row_hot, firing[s : s + 1], 0.0) for s in shot_range]
    placed = spread(jnp.concatenate(lefts, axis=0).astype(BF16))
    tally[...] = placed[:cells].reshape(planes, rows, cols)
    fired[...] = placed[cells:].reshape(shots, planes, rows, cols)

    def record(k):
        lefts = []
        for s in shot_range:
            row = recordings[s, k : k + 1, :]
            high = row.astype(BF16).astype(F32)
            lefts.append(jnp.where(row_hot, high, 0.0).astype(BF16))
            lefts.append(jnp.where(row_hot, row - high, 0.0).astype(BF16))
        both = spread(jnp.concatenate(lefts, axis=0)).reshape(shots, 2, planes, rows, cols)
        recorded[k] = both[:, 0] + both[:, 1]

    row_at = lax.broadcasted_iota(jnp.int32, (rows, cols), 0)
    col_at = lax.broadcasted_iota(jnp.int32, (rows, cols), 1)

    def inner(earlier, current, s, z):
        x = current[s, z].astype(F32)
        around = jnp.where(row_at == rows - 1, 0.0, pltpu.roll(x, rows - 1, 0))
        around += jnp.where(row_at == 0, 0.0, pltpu.roll(x, 1, 0))
        around += jnp.where(col_at == cols - 1, 0.0, pltpu.roll(x, cols - 1, 1))
        around += jnp.where(col_at == 0, 0.0, pltpu.roll(x, 1, 1))
        if z < last:
            around += current[s, z + 1].astype(F32)
        if z > 0:
            around += current[s, z - 1].astype(F32)
        return 2.0 * x - earlier[s, z].astype(F32) + courant[z] * (around - 6.0 * x)

    order = [0] + ([last] if last else []) + list(range(1, last))

    def finish(fields, link, j, moving):
        following = fields[j + 2]
        for z in order:
            if z == 0:
                receive(0, fields[j + 1], *link, j)
            if z == last:
                receive(1, fields[j + 1], *link, j)
            for s in shot_range:
                value = partial[s, z]
                if z == 0:
                    value += courant[z] * link[0][0, j, s].astype(F32)
                if z == last:
                    value += courant[z] * link[0][1, j, s].astype(F32)
                following[s, z] = value.astype(BF16)
            if moving and z == 0:
                send(1, following, *link, j + 1)
            if moving and z == last:
                send(0, following, *link, j + 1)

    def start_forward(j):
        for s in shot_range:
            for z in plane_range:
                partial[s, z] = (
                    inner(ahead[j], ahead[j + 1], s, z) + signature[j] * fired[s, z]
                )

    def correlate(k):
        for s in shot_range:
            top, bottom = 0.0, 0.0
            for z in plane_range:
                p = ahead[k + 2][s, z].astype(F32)
                top += p * recorded[k, s, z]
                bottom += p * p * tally[z]
            if k:
                top += products[s, 0]
                bottom += products[s, 1]
            products[s, 0] = top
            products[s, 1] = bottom

    start_forward(0)
    for j in range(ticks):
        finish(ahead, ahead_link, j, j < ticks - 1)
        if j < ticks - 1:
            start_forward(j + 1)
            record(j)
            correlate(j)
            if j == ticks - 2:
                record(ticks - 1)
        else:
            correlate(j)

    line = lax.broadcasted_iota(jnp.int32, (8, 128), 0)
    block = jnp.zeros((8, 128), F32)
    for s in shot_range:
        block = jnp.where(line == 2 * s, jnp.sum(products[s, 0]), block)
        block = jnp.where(line == 2 * s + 1, jnp.sum(products[s, 1]), block)
    sums[...] = block

    def share(d):
        return pltpu.make_async_remote_copy(
            src_ref=sums,
            dst_ref=gathered.at[me],
            send_sem=sums_sent.at[d],
            recv_sem=sums_got.at[me],
            device_id={"space": lax.rem(me + d, peers)},
            device_id_type=MESH,
        )

    def shared(d):
        other = lax.rem(me + d, peers)
        return pltpu.make_async_remote_copy(
            src_ref=sums,
            dst_ref=gathered.at[other],
            send_sem=sums_sent.at[d],
            recv_sem=sums_got.at[other],
            device_id={"space": other},
            device_id_type=MESH,
        )

    for d in range(1, peers):
        share(d).start()
    gathered[me] = block

    for s in shot_range:
        for z in plane_range:
            partial[s, z] = inner(beyond, terminal, s, z) - recorded[ticks - 1, s, z]

    for d in range(1, peers):
        shared(d).wait_recv()
    whole = gathered[0]
    for i in range(1, peers):
        whole += gathered[i]
    scales = []
    for s in shot_range:
        scale = whole[2 * s : 2 * s + 1] / (whole[2 * s + 1 : 2 * s + 2] + EPSILON)
        scales.append(scale[:, :1])
        amplitude[s] = jnp.max(scale)

    for s in shot_range:
        for z in plane_range:
            p = final[s, z].astype(F32)
            partial[s, z] = partial[s, z] + scales[s] * (tally[z] * p)

    def gather_total(j, z):
        moment = ticks - 1 - j
        value = 0.0
        for s in shot_range:
            curvature = (
                ahead[moment + 2][s, z].astype(F32)
                - 2.0 * ahead[moment + 1][s, z].astype(F32)
                + ahead[moment][s, z].astype(F32)
            )
            value += back[j + 2][s, z].astype(F32) * curvature
        return value if j == 0 else total[z] + value

    def swap(z):
        return pltpu.make_async_remote_copy(
            src_ref=outgoing.at[z],
            dst_ref=incoming.at[z],
            send_sem=total_sent.at[z],
            recv_sem=total_got.at[z],
            device_id={"shot": 1 - core},
            device_id_type=MESH,
        )

    for j in range(ticks):
        finish(back, back_link, j, j < ticks - 1)
        if j < ticks - 1:
            k = ticks - 2 - j
            for s in shot_range:
                for z in plane_range:
                    source = scales[s] * (tally[z] * ahead[k + 2][s, z].astype(F32))
                    partial[s, z] = (
                        inner(back[j + 1], back[j + 2], s, z) + source - recorded[k, s, z]
                    )
            for z in plane_range:
                total[z] = gather_total(j, z)
        else:
            for z in plane_range:
                outgoing[z] = gather_total(j, z).astype(BF16)
                swap(z).start()

    weight = 2.0 * (1500.0 / velocity[...]) ** 3
    for z in plane_range:
        swap(z).wait_recv()
        gradient[z] = weight[z] * (outgoing[z].astype(F32) + incoming[z].astype(F32))

    for fields, link in ((ahead, ahead_link), (back, back_link)):
        for j in range(ticks):
            for side in (0, 1):
                drain(side, fields[j + 1], *link, j)
    for d in range(1, peers):
        share(d).wait_send()
    for z in plane_range:
        swap(z).wait_send()


def body(peers, *args):
    medium, entry, locations, recordings = args[0], args[2], args[7], args[8]
    shots, planes, rows, cols = entry.shape
    ticks = recordings.shape[1]
    probes = locations.shape[1]
    vmem = pl.BlockSpec(memory_space=pltpu.VMEM)
    smem = pl.BlockSpec(memory_space=pltpu.SMEM)
    slab = (planes, rows, cols)
    dma = pltpu.SemaphoreType.DMA
    return pl.pallas_call(
        functools.partial(kernel, peers),
        out_shape=(
            jax.ShapeDtypeStruct(entry.shape, BF16),
            jax.ShapeDtypeStruct((shots,), F32),
            jax.ShapeDtypeStruct(medium.shape, F32),
        ),
        in_specs=[vmem] * 5 + [smem] + [vmem] * 3,
        out_specs=(vmem, smem, vmem),
        scratch_shapes=[
            pltpu.VMEM((ticks - 1, shots) + slab, BF16),
            pltpu.VMEM((ticks, shots) + slab, BF16),
            pltpu.VMEM((2, ticks, shots, rows, cols), BF16),
            pltpu.VMEM((2, ticks, shots, rows, cols), BF16),
            pltpu.VMEM(slab, F32),
            pltpu.VMEM((shots,) + slab, F32),
            pltpu.VMEM((cols, probes), BF16),
            pltpu.VMEM(slab, F32),
            pltpu.VMEM((shots,) + slab, F32),
            pltpu.VMEM((ticks, shots) + slab, F32),
            pltpu.VMEM((8, 128), F32),
            pltpu.VMEM((shots, 2, rows, cols), F32),
            pltpu.VMEM((peers, 8, 128), F32),
            pltpu.VMEM(slab, F32),
            pltpu.VMEM(slab, BF16),
            pltpu.VMEM(slab, BF16),
            dma((2, ticks)),
            dma((2, ticks)),
            dma((2, ticks)),
            dma((2, ticks)),
            dma((peers,)),
            dma((peers,)),
            dma((planes,)),
            dma((planes,)),
        ],
        compiler_params=pltpu.CompilerParams(
            collective_id=0, has_side_effects=True, vmem_limit_bytes=40 * 1024 * 1024
        ),
    )(*args)


def solution(mesh):
    placed = (
        P("space", None, None),
        P("shot", "space", None, None),
        P("shot", "space", None, None),
        P("shot", "space", None, None),
        P("shot", "space", None, None),
        P(),
        P("shot", None),
        P(),
        P("shot", None, None),
    )
    return jax.shard_map(
        functools.partial(body, mesh.shape["space"]),
        mesh=mesh,
        in_specs=placed,
        out_specs=(P("shot", "space", None, None), P("shot"), P("space", None, None)),
        check_vma=False,
    )
```

time: 840 us -> 73.5 us (0.09)
  the two profiles are of different devices: /device:TPU:0 before, /device:TPU:7 now
where the time goes in v1:
time: 73.5 us; the launch traced here: 73.2 us
  Pallas kernels  65.3 us (89%)
  local copies, waits for them, and re-layouts  7.19 us (10%)
    pallas_call x1, Pallas kernels, body(): pl.pallas_call(functools.partial(kernel, peers), out_shape=(jax.ShapeDtyp...  65.3 us
    unnamed x20, local copies, waits for them, and re-layouts  7.19 us

profile of v1, /device:TPU:7, one launch (start us, length us, event | category | flops | bytes accessed | tf_op | source)
XLA Modules:
  0.0 73.2 jit_solution(7783828310641518713)
XLA Ops:
  0.6 0.0 copy-start.5
  0.6 0.0 copy-start.6
  0.7 0.0 copy-start.7
  0.7 0.8 %copy.12.recordings = f32[2,6,1024]{2,1,0:T(8,128)S(1)} copy(f32[2,6,1024]{2,0,1:T(2,128)} %param.17) | data formatting | bytes 98304 | tf_op args[8]
  1.5 0.0 copy-done.5
  1.5 0.0 copy-done.6
  1.5 0.0 copy-done.7
  1.5 0.0 copy-start
  1.5 0.9 %copy-done = f32[2,32,512]{2,1,0:T(8,128)S(1)} copy-done((f32[2,32,512]{2,1,0:T(8,128)S(1)}, f32[2,32,512]{2,1,0:T(8,128)}, u32[]{:S(2)}) %copy-start) | copy-done | bytes 131096
  2.4 0.0 copy-start.1
  2.4 0.9 %copy-done.1 = bf16[2,2,32,512]{3,2,1,0:T(8,128)(2,1)S(1)} copy-done((bf16[2,2,32,512]{3,2,1,0:T(8,128)(2,1)S(1)}, bf16[2,2,32,512]{3,2,1,0:T(8,128)(2,1)}, u32[]{:S(2)}) %copy-start.1) | copy-done | bytes 131096
  3.3 0.0 copy-start.2
  3.3 0.9 %copy-done.2 = bf16[2,2,32,512]{3,2,1,0:T(8,128)(2,1)S(1)} copy-done((bf16[2,2,32,512]{3,2,1,0:T(8,128)(2,1)S(1)}, bf16[2,2,32,512]{3,2,1,0:T(8,128)(2,1)}, u32[]{:S(2)}) %copy-start.2) | copy-done | bytes 131096
  4.2 0.0 copy-start.3
  4.2 0.9 %copy-done.3 = bf16[2,2,32,512]{3,2,1,0:T(8,128)(2,1)S(1)} copy-done((bf16[2,2,32,512]{3,2,1,0:T(8,128)(2,1)S(1)}, bf16[2,2,32,512]{3,2,1,0:T(8,128)(2,1)}, u32[]{:S(2)}) %copy-start.3) | copy-done | bytes 131096
  5.2 0.0 copy-start.4
  5.2 0.9 %copy-done.4 = bf16[2,2,32,512]{3,2,1,0:T(8,128)(2,1)S(1)} copy-done((bf16[2,2,32,512]{3,2,1,0:T(8,128)(2,1)S(1)}, bf16[2,2,32,512]{3,2,1,0:T(8,128)(2,1)}, u32[]{:S(2)}) %copy-start.4) | copy-done | bytes 131096
  6.1 65.3 %shard_map.112 = (bf16[2,2,32,512]{3,2,1,0:T(8,128)(2,1)S(1)}, f32[2]{0:T(128)S(1)}, f32[2,32,512]{2,1,0:T(8,128)S(1)}) custom-call(f32[2,32,512]{2,1,0:T(8,128)S(1)} %copy-done, bf16[2,2,32,512]{3,2,1,0:T(8,128)(2,1)S(1)} %copy-done.1, bf16[2,2,32,512]{3,2,1,0:T(8,128)(2,1)S(1)} %copy-done.2, bf16[2,2,32,512]{3,2,1,0:T(8,128)(2,1)S(1)} %copy-done.3, ...), custom_call_target="tpu_custom_call" | custom-call | tf_op jit(solution)/shard_map/pallas_call | solution.py:334
  71.4 0.7 copy.16
  72.0 0.5 copy.17
  72.6 0.7 copy.18
Async XLA Ops:
  0.6 0.9 %copy-start.5 = (s32[3,1024]{1,0:T(4,128)S(1)}, s32[3,1024]{1,0:T(4,128)}, u32[]{:S(2)}) copy-start(s32[3,1024]{1,0:T(4,128)} %locations.1) | copy-start | bytes 36868
  0.6 0.9 %copy-start.6 = (s32[2,1024]{1,0:T(2,128)S(1)}, s32[2,1024]{1,0:T(2,128)}, u32[]{:S(2)}) copy-start(s32[2,1024]{1,0:T(2,128)} %emitters.1) | copy-start | bytes 24580
  0.7 0.9 %copy-start.7 = (f32[6]{0:T(128)S(1)}, f32[6]{0:T(128)}, u32[]{:S(2)}) copy-start(f32[6]{0:T(128)} %signature.1) | copy-start | bytes 76
  1.5 0.9 %copy-start = (f32[2,32,512]{2,1,0:T(8,128)S(1)}, f32[2,32,512]{2,1,0:T(8,128)}, u32[]{:S(2)}) copy-start(f32[2,32,512]{2,1,0:T(8,128)} %velocity.1) | copy-start | bytes 393220
  2.4 0.9 %copy-start.1 = (bf16[2,2,32,512]{3,2,1,0:T(8,128)(2,1)S(1)}, bf16[2,2,32,512]{3,2,1,0:T(8,128)(2,1)}, u32[]{:S(2)}) copy-start(bf16[2,2,32,512]{3,2,1,0:T(8,128)(2,1)} %preceding.1) | copy-start | bytes 393220
  3.3 0.9 %copy-start.2 = (bf16[2,2,32,512]{3,2,1,0:T(8,128)(2,1)S(1)}, bf16[2,2,32,512]{3,2,1,0:T(8,128)(2,1)}, u32[]{:S(2)}) copy-start(bf16[2,2,32,512]{3,2,1,0:T(8,128)(2,1)} %entry.1) | copy-start | bytes 393220
  4.2 0.9 %copy-start.3 = (bf16[2,2,32,512]{3,2,1,0:T(8,128)(2,1)S(1)}, bf16[2,2,32,512]{3,2,1,0:T(8,128)(2,1)}, u32[]{:S(2)}) copy-start(bf16[2,2,32,512]{3,2,1,0:T(8,128)(2,1)} %beyond.1) | copy-start | bytes 393220
  5.2 0.9 %copy-start.4 = (bf16[2,2,32,512]{3,2,1,0:T(8,128)(2,1)S(1)}, bf16[2,2,32,512]{3,2,1,0:T(8,128)(2,1)}, u32[]{:S(2)}) copy-start(bf16[2,2,32,512]{3,2,1,0:T(8,128)(2,1)} %terminal.1) | copy-start | bytes 393220

commit v2 on v1

v2 whole, which is shorter than its diff:
```python
import functools

import jax
import jax.numpy as jnp
from jax import lax
from jax.experimental import pallas as pl
from jax.experimental.pallas import tpu as pltpu
from jax.sharding import PartitionSpec as P

SPEED_SCALE = 1.0 / 6000.0
EPSILON = 1e-06
MESH = pl.DeviceIdType.MESH
F32 = jnp.float32
BF16 = jnp.bfloat16


def kernel(
    peers,
    velocity_in,
    preceding_in,
    entry_in,
    beyond_in,
    terminal_in,
    signature,
    emitters,
    locations,
    recordings,
    final,
    amplitude,
    gradient,
    velocity,
    preceding,
    entry,
    beyond,
    terminal,
    forward,
    backward,
    forward_halo,
    backward_halo,
    forward_ring,
    backward_ring,
    preceding_ring,
    beyond_ring,
    final_ring,
    velocity_ring,
    courant,
    courant_ring,
    partial,
    column_hot,
    tally,
    fired,
    recorded,
    sums,
    products,
    gathered,
    total,
    outgoing,
    incoming,
    loaded,
    forward_sent,
    forward_got,
    backward_sent,
    backward_got,
    preceding_sent,
    preceding_got,
    beyond_sent,
    beyond_got,
    final_sent,
    final_got,
    velocity_sent,
    velocity_got,
    sums_sent,
    sums_got,
    total_sent,
    total_got,
):
    me = lax.axis_index("space")
    core = lax.axis_index("shot")
    shots, planes, rows, cols = entry.shape
    ticks = recordings.shape[1]
    last = planes - 1
    shot_range, plane_range, sides = range(shots), range(planes), (0, 1)
    pairs = ticks // 2

    barrier = pltpu.get_barrier_semaphore()
    for d in range(1, peers):
        pl.semaphore_signal(
            barrier, inc=1, device_id={"space": lax.rem(me + d, peers)}, device_id_type=MESH
        )
    pl.semaphore_signal(barrier, inc=1, device_id={"shot": 1 - core}, device_id_type=MESH)

    loads = [
        pltpu.make_async_copy(source, target, loaded.at[i])
        for i, (source, target) in enumerate(
            (
                (velocity_in, velocity),
                (preceding_in, preceding),
                (entry_in, entry),
                (beyond_in, beyond),
                (terminal_in, terminal),
            )
        )
    ]
    for load in loads:
        load.start()

    pl.semaphore_wait(barrier, peers)

    def hop(side, source, target, sent, got):
        return pltpu.make_async_remote_copy(
            src_ref=source,
            dst_ref=target,
            send_sem=sent,
            recv_sem=got,
            device_id={"space": me + 1 if side == 0 else me - 1},
            device_id_type=MESH,
        )

    started = []

    def send(side, *args):
        @pl.when(me < peers - 1 if side == 0 else me > 0)
        def _():
            hop(side, *args).start()

        started.append((side, args))

    def receive(side, *args):
        @pl.when(me > 0 if side == 0 else me < peers - 1)
        def _():
            hop(side, *args).wait_recv()

    def pair_args(side, field, link, e, s):
        halo, sent, got = link
        low = planes - 2 if side == 0 else 0
        return (
            field.at[s, pl.ds(low, 2)],
            halo.at[side, e, s],
            sent.at[side, e, s],
            got.at[side, e, s],
        )

    def plane_args(side, field, ring, sent, got, s):
        edge = last if side == 0 else 0
        return field.at[s, edge], ring.at[side, s], sent.at[side, s], got.at[side, s]

    def velocity_args(side):
        edge = last if side == 0 else 0
        return (
            velocity_in.at[edge],
            velocity_ring.at[side],
            velocity_sent.at[side],
            velocity_got.at[side],
        )

    ahead = [preceding, entry] + [forward.at[j] for j in range(ticks - 1)] + [final]
    back = [beyond, terminal] + [backward.at[j] for j in range(ticks)]
    ahead_link = (forward_halo, forward_sent, forward_got)
    back_link = (backward_halo, backward_sent, backward_got)
    preceding_link = (preceding_ring, preceding_sent, preceding_got)
    beyond_link = (beyond_ring, beyond_sent, beyond_got)
    final_link = (final_ring, final_sent, final_got)

    for s in shot_range:
        for side in sides:
            send(side, *pair_args(side, entry_in, ahead_link, 0, s))
        for side in sides:
            send(side, *plane_args(side, preceding_in, *preceding_link, s))
        if s == 0:
            for side in sides:
                send(side, *velocity_args(side))
    for s in shot_range:
        for side in sides:
            send(side, *pair_args(side, terminal_in, back_link, 0, s))
        for side in sides:
            send(side, *plane_args(side, beyond_in, *beyond_link, s))

    for side, here in ((0, me == 0), (1, me == peers - 1)):

        @pl.when(here)
        def _(side=side):
            for ring in (
                forward_halo,
                backward_halo,
                preceding_ring,
                beyond_ring,
                final_ring,
                velocity_ring,
            ):
                ring[side] = jnp.zeros_like(ring[side])

    probes = locations.shape[1]
    wide = planes + 2
    cells = wide * rows
    row_of = (locations[0:1, :] - me * planes + 1) * rows + locations[1:2, :]
    row_hot = lax.broadcasted_iota(jnp.int32, (cells, probes), 0) == row_of
    column_hot[...] = jnp.where(
        lax.broadcasted_iota(jnp.int32, (cols, probes), 0) == locations[2:3, :], 1.0, 0.0
    ).astype(BF16)

    def spread(left):
        return lax.dot_general(
            left, column_hot[...], (((1,), (1,)), ((), ())), preferred_element_type=F32
        )

    firing = emitters[...].astype(F32)
    lefts = [jnp.where(row_hot, 1.0, 0.0)]
    lefts += [jnp.where(row_hot, firing[s : s + 1], 0.0) for s in shot_range]
    placed = spread(jnp.concatenate(lefts, axis=0).astype(BF16))
    tally[...] = placed[:cells].reshape(wide, rows, cols)
    fired[...] = placed[cells:].reshape(shots, wide, rows, cols)

    def record(k):
        for s in shot_range:
            row = recordings[s, k : k + 1, :]
            high = row.astype(BF16).astype(F32)
            lefts = [
                jnp.where(row_hot, high, 0.0).astype(BF16),
                jnp.where(row_hot, row - high, 0.0).astype(BF16),
            ]
            both = spread(jnp.concatenate(lefts, axis=0)).reshape(2, wide, rows, cols)
            recorded[k, s] = both[0] + both[1]

    row_at = lax.broadcasted_iota(jnp.int32, (rows, cols), 0)
    col_at = lax.broadcasted_iota(jnp.int32, (rows, cols), 1)

    def in_plane(x):
        around = jnp.where(row_at == rows - 1, 0.0, pltpu.roll(x, rows - 1, 0))
        around += jnp.where(row_at == 0, 0.0, pltpu.roll(x, 1, 0))
        around += jnp.where(col_at == cols - 1, 0.0, pltpu.roll(x, cols - 1, 1))
        around += jnp.where(col_at == 0, 0.0, pltpu.roll(x, 1, 1))
        return around

    def inner(earlier, current, s, z):
        x = current[s, z].astype(F32)
        around = in_plane(x)
        if z < last:
            around += current[s, z + 1].astype(F32)
        if z > 0:
            around += current[s, z - 1].astype(F32)
        return 2.0 * x - earlier[s, z].astype(F32) + courant[z] * (around - 6.0 * x)

    def near(halo, side, e, s):
        return halo[side, e, s, 1 - side]

    def begin(fields, e, s, source):
        for z in plane_range:
            partial[s, z] = inner(fields[2 * e], fields[2 * e + 1], s, z) + source(
                2 * e, s, z + 1, fields
            )

    def two_steps(fields, link, rings, e, s, before, source, ring_source):
        halo = link[0]
        j = 2 * e
        earlier, current, middle, after = fields[j : j + 4]
        for z in plane_range:
            value = partial[s, z]
            if z == 0:
                value += courant[z] * near(halo, 0, e, s).astype(F32)
            if z == last:
                value += courant[z] * near(halo, 1, e, s).astype(F32)
            middle[s, z] = value.astype(BF16)
        for side in sides:
            x = near(halo, side, e, s).astype(F32)
            around = in_plane(x) + halo[side, e, s, side].astype(F32)
            around += current[s, 0 if side == 0 else last].astype(F32)
            old = before[side, s] if e == 0 else rings[side, e - 1, s]
            value = 2.0 * x - old.astype(F32) + courant_ring[side] * (around - 6.0 * x)
            rings[side, e, s] = (value + ring_source(e, s, side)).astype(BF16)
        for z in plane_range:
            value = inner(current, middle, s, z) + source(j + 1, s, z + 1, fields)
            if z == 0:
                value += courant[z] * rings[0, e, s].astype(F32)
            if z == last:
                value += courant[z] * rings[1, e, s].astype(F32)
            after[s, z] = value.astype(BF16)
        if e < pairs - 1:
            for side in sides:
                send(side, *pair_args(side, after, link, e + 1, s))

    def fire(j, s, w, fields):
        return signature[j] * fired[s, w]

    def fire_ring(e, s, side):
        return signature[2 * e] * fired[s, 0 if side == 0 else wide - 1]

    def correlate(k, s):
        top, bottom = 0.0, 0.0
        for z in plane_range:
            p = ahead[k + 2][s, z].astype(F32)
            top += p * recorded[k, s, z + 1]
            bottom += p * p * tally[z + 1]
        if k:
            top += products[s, 0]
            bottom += products[s, 1]
        products[s, 0] = top
        products[s, 1] = bottom

    for load in loads:
        load.wait()
    courant[...] = (velocity[...] * SPEED_SCALE) ** 2
    for s in shot_range:
        begin(ahead, 0, s, fire)
    for k in range(ticks):
        record(k)
    for side in sides:
        receive(side, *velocity_args(side))
    courant_ring[...] = (velocity_ring[...] * SPEED_SCALE) ** 2

    for e in range(pairs):
        for s in shot_range:
            for side in sides:
                receive(side, *pair_args(side, ahead[2 * e + 1], ahead_link, e, s))
            if e == 0:
                for side in sides:
                    receive(side, *plane_args(side, preceding_in, *preceding_link, s))
            two_steps(
                ahead, ahead_link, forward_ring, e, s, preceding_ring, fire, fire_ring
            )
            if e < pairs - 1:
                begin(ahead, e + 1, s, fire)
            else:
                for side in sides:
                    send(side, *plane_args(side, final, *final_link, s))
            correlate(2 * e, s)
            correlate(2 * e + 1, s)

    line = lax.broadcasted_iota(jnp.int32, (8, 128), 0)
    block = jnp.zeros((8, 128), F32)
    for s in shot_range:
        block = jnp.where(line == 2 * s, jnp.sum(products[s, 0]), block)
        block = jnp.where(line == 2 * s + 1, jnp.sum(products[s, 1]), block)
    sums[...] = block

    def share(d):
        return pltpu.make_async_remote_copy(
            src_ref=sums,
            dst_ref=gathered.at[me],
            send_sem=sums_sent.at[d],
            recv_sem=sums_got.at[me],
            device_id={"space": lax.rem(me + d, peers)},
            device_id_type=MESH,
        )

    def shared(d):
        other = lax.rem(me + d, peers)
        return pltpu.make_async_remote_copy(
            src_ref=sums,
            dst_ref=gathered.at[other],
            send_sem=sums_sent.at[d],
            recv_sem=sums_got.at[other],
            device_id={"space": other},
            device_id_type=MESH,
        )

    for d in range(1, peers):
        share(d).start()
    gathered[me] = block

    for s in shot_range:
        begin(back, 0, s, lambda j, s, w, fields: -recorded[ticks - 1, s, w])
        for side in sides:
            receive(side, *pair_args(side, terminal_in, back_link, 0, s))
            receive(side, *plane_args(side, beyond_in, *beyond_link, s))
            receive(side, *plane_args(side, final, *final_link, s))

    for d in range(1, peers):
        shared(d).wait_recv()
    whole = gathered[0]
    for i in range(1, peers):
        whole += gathered[i]
    scales = []
    for s in shot_range:
        scale = whole[2 * s : 2 * s + 1] / (whole[2 * s + 1 : 2 * s + 2] + EPSILON)
        scales.append(scale[:, :1])
        amplitude[s] = jnp.max(scale)

    for s in shot_range:
        for z in plane_range:
            p = final[s, z].astype(F32)
            partial[s, z] = partial[s, z] + scales[s] * (tally[z + 1] * p)

    def residue(j, s, w, fields):
        k = ticks - 1 - j
        p = ahead[k + 2][s, w - 1].astype(F32)
        return scales[s] * (tally[w] * p) - recorded[k, s, w]

    def residue_ring(e, s, side):
        w = 0 if side == 0 else wide - 1
        p = final_ring[side, s] if e == 0 else near(forward_halo, side, pairs - e, s)
        return scales[s] * (tally[w] * p.astype(F32)) - recorded[ticks - 1 - 2 * e, s, w]

    def gather_total(j, z):
        moment = ticks - 1 - j
        value = 0.0
        for s in shot_range:
            curvature = (
                ahead[moment + 2][s, z].astype(F32)
                - 2.0 * ahead[moment + 1][s, z].astype(F32)
                + ahead[moment][s, z].astype(F32)
            )
            value += back[j + 2][s, z].astype(F32) * curvature
        return value if j == 0 else total[z] + value

    def swap(z):
        return pltpu.make_async_remote_copy(
            src_ref=outgoing.at[z],
            dst_ref=incoming.at[z],
            send_sem=total_sent.at[z],
            recv_sem=total_got.at[z],
            device_id={"shot": 1 - core},
            device_id_type=MESH,
        )

    for e in range(pairs):
        for s in shot_range:
            if e:
                for side in sides:
                    receive(side, *pair_args(side, back[2 * e + 1], back_link, e, s))
            two_steps(
                back, back_link, backward_ring, e, s, beyond_ring, residue, residue_ring
            )
            if e < pairs - 1:
                begin(back, e + 1, s, residue)
        for z in plane_range:
            total[z] = gather_total(2 * e, z)
            value = gather_total(2 * e + 1, z)
            if e < pairs - 1:
                total[z] = value
            else:
                outgoing[z] = value.astype(BF16)
                swap(z).start()

    for z in plane_range:
        weight = 2.0 * (1500.0 / velocity[z]) ** 3
        swap(z).wait_recv()
        gradient[z] = weight * (outgoing[z].astype(F32) + incoming[z].astype(F32))

    for side, args in started:

        @pl.when(me < peers - 1 if side == 0 else me > 0)
        def _(side=side, args=args):
            hop(side, *args).wait_send()

    for d in range(1, peers):
        share(d).wait_send()
    for z in plane_range:
        swap(z).wait_send()


def body(peers, *args):
    medium, entry, locations, recordings = args[0], args[2], args[7], args[8]
    shots, planes, rows, cols = entry.shape
    ticks = recordings.shape[1]
    probes = locations.shape[1]
    vmem = pl.BlockSpec(memory_space=pltpu.VMEM)
    smem = pl.BlockSpec(memory_space=pltpu.SMEM)
    slab = (planes, rows, cols)
    wide = (planes + 2, rows, cols)
    pairs = ticks // 2
    dma = pltpu.SemaphoreType.DMA
    return pl.pallas_call(
        functools.partial(kernel, peers),
        out_shape=(
            jax.ShapeDtypeStruct(entry.shape, BF16),
            jax.ShapeDtypeStruct((shots,), F32),
            jax.ShapeDtypeStruct(medium.shape, F32),
        ),
        in_specs=[pl.BlockSpec(memory_space=pl.ANY)] * 5 + [smem] + [vmem] * 3,
        out_specs=(vmem, smem, vmem),
        scratch_shapes=[
            pltpu.VMEM(slab, F32),
            pltpu.VMEM((shots,) + slab, BF16),
            pltpu.VMEM((shots,) + slab, BF16),
            pltpu.VMEM((shots,) + slab, BF16),
            pltpu.VMEM((shots,) + slab, BF16),
            pltpu.VMEM((ticks - 1, shots) + slab, BF16),
            pltpu.VMEM((ticks, shots) + slab, BF16),
            pltpu.VMEM((2, pairs, shots, 2, rows, cols), BF16),
            pltpu.VMEM((2, pairs, shots, 2, rows, cols), BF16),
            pltpu.VMEM((2, pairs, shots, rows, cols), BF16),
            pltpu.VMEM((2, pairs, shots, rows, cols), BF16),
            pltpu.VMEM((2, shots, rows, cols), BF16),
            pltpu.VMEM((2, shots, rows, cols), BF16),
            pltpu.VMEM((2, shots, rows, cols), BF16),
            pltpu.VMEM((2, rows, cols), F32),
            pltpu.VMEM(slab, F32),
            pltpu.VMEM((2, rows, cols), F32),
            pltpu.VMEM((shots,) + slab, F32),
            pltpu.VMEM((cols, probes), BF16),
            pltpu.VMEM(wide, F32),
            pltpu.VMEM((shots,) + wide, F32),
            pltpu.VMEM((ticks, shots) + wide, F32),
            pltpu.VMEM((8, 128), F32),
            pltpu.VMEM((shots, 2, rows, cols), F32),
            pltpu.VMEM((peers, 8, 128), F32),
            pltpu.VMEM(slab, F32),
            pltpu.VMEM(slab, BF16),
            pltpu.VMEM(slab, BF16),
            dma((5,)),
            dma((2, pairs, shots)),
            dma((2, pairs, shots)),
            dma((2, pairs, shots)),
            dma((2, pairs, shots)),
            dma((2, shots)),
            dma((2, shots)),
            dma((2, shots)),
            dma((2, shots)),
            dma((2, shots)),
            dma((2, shots)),
            dma((2,)),
            dma((2,)),
            dma((peers,)),
            dma((peers,)),
            dma((planes,)),
            dma((planes,)),
        ],
        compiler_params=pltpu.CompilerParams(
            collective_id=0, has_side_effects=True, vmem_limit_bytes=40 * 1024 * 1024
        ),
    )(*args)


def solution(mesh):
    placed = (
        P("space", None, None),
        P("shot", "space", None, None),
        P("shot", "space", None, None),
        P("shot", "space", None, None),
        P("shot", "space", None, None),
        P(),
        P("shot", None),
        P(),
        P("shot", None, None),
    )
    return jax.shard_map(
        functools.partial(body, mesh.shape["space"]),
        mesh=mesh,
        in_specs=placed,
        out_specs=(P("shot", "space", None, None), P("shot"), P("space", None, None)),
        check_vma=False,
    )
```

time: 73.5 us -> 69.8 us (0.950)
  the two profiles are of different devices: /device:TPU:7 before, /device:TPU:0 now
where the time goes in v2:
time: 69.8 us; the launch traced here: 69.6 us
  Pallas kernels  61.7 us (88%)
  local copies, waits for them, and re-layouts  7.19 us (10%)
  between operations  0.7 us (1%)
    pallas_call x1, Pallas kernels, body(): pl.pallas_call(functools.partial(kernel, peers), out_shape=(jax.ShapeDtyp...  61.7 us
    unnamed x20, local copies, waits for them, and re-layouts  7.19 us

profile of v2, /device:TPU:0, one launch (start us, length us, event | category | flops | bytes accessed | tf_op | source)
XLA Modules:
  0.0 69.6 jit_solution(12748799604104765188)
XLA Ops:
  0.6 0.0 copy-start.5
  0.6 0.0 copy-start.6
  0.7 0.0 copy-start.7
  0.7 0.8 %copy.12.recordings = f32[2,6,1024]{2,1,0:T(8,128)S(1)} copy(f32[2,6,1024]{2,0,1:T(2,128)} %param.17) | data formatting | bytes 98304 | tf_op args[8]
  1.5 0.0 copy-done.5
  1.5 0.0 copy-done.6
  1.5 0.0 copy-done.7
  1.5 0.0 copy-start
  1.5 0.9 %copy-done = f32[2,32,512]{2,1,0:T(8,128)S(1)} copy-done((f32[2,32,512]{2,1,0:T(8,128)S(1)}, f32[2,32,512]{2,1,0:T(8,128)}, u32[]{:S(2)}) %copy-start) | copy-done | bytes 131096
  2.4 0.0 copy-start.1
  2.4 0.9 %copy-done.1 = bf16[2,2,32,512]{3,2,1,0:T(8,128)(2,1)S(1)} copy-done((bf16[2,2,32,512]{3,2,1,0:T(8,128)(2,1)S(1)}, bf16[2,2,32,512]{3,2,1,0:T(8,128)(2,1)}, u32[]{:S(2)}) %copy-start.1) | copy-done | bytes 131096
  3.3 0.0 copy-start.2
  3.3 0.9 %copy-done.2 = bf16[2,2,32,512]{3,2,1,0:T(8,128)(2,1)S(1)} copy-done((bf16[2,2,32,512]{3,2,1,0:T(8,128)(2,1)S(1)}, bf16[2,2,32,512]{3,2,1,0:T(8,128)(2,1)}, u32[]{:S(2)}) %copy-start.2) | copy-done | bytes 131096
  4.2 0.0 copy-start.3
  4.2 0.9 %copy-done.3 = bf16[2,2,32,512]{3,2,1,0:T(8,128)(2,1)S(1)} copy-done((bf16[2,2,32,512]{3,2,1,0:T(8,128)(2,1)S(1)}, bf16[2,2,32,512]{3,2,1,0:T(8,128)(2,1)}, u32[]{:S(2)}) %copy-start.3) | copy-done | bytes 131096
  5.2 0.0 copy-start.4
  5.2 0.9 %copy-done.4 = bf16[2,2,32,512]{3,2,1,0:T(8,128)(2,1)S(1)} copy-done((bf16[2,2,32,512]{3,2,1,0:T(8,128)(2,1)S(1)}, bf16[2,2,32,512]{3,2,1,0:T(8,128)(2,1)}, u32[]{:S(2)}) %copy-start.4) | copy-done | bytes 131096
  6.1 61.7 %shard_map.112 = (bf16[2,2,32,512]{3,2,1,0:T(8,128)(2,1)S(1)}, f32[2]{0:T(128)S(1)}, f32[2,32,512]{2,1,0:T(8,128)S(1)}) custom-call(f32[2,32,512]{2,1,0:T(8,128)S(1)} %copy-done, bf16[2,2,32,512]{3,2,1,0:T(8,128)(2,1)S(1)} %copy-done.1, bf16[2,2,32,512]{3,2,1,0:T(8,128)(2,1)S(1)} %copy-done.2, bf16[2,2,32,512]{3,2,1,0:T(8,128)(2,1)S(1)} %copy-done.3, ...), custom_call_target="tpu_custom_call" | custom-call | tf_op jit(solution)/shard_map/pallas_call | solution.py:462
  67.7 0.7 copy.16
  68.4 0.5 copy.17
  68.9 0.7 copy.18
Async XLA Ops:
  0.6 0.9 %copy-start.5 = (s32[3,1024]{1,0:T(4,128)S(1)}, s32[3,1024]{1,0:T(4,128)}, u32[]{:S(2)}) copy-start(s32[3,1024]{1,0:T(4,128)} %locations.1) | copy-start | bytes 36868
  0.6 0.9 %copy-start.6 = (s32[2,1024]{1,0:T(2,128)S(1)}, s32[2,1024]{1,0:T(2,128)}, u32[]{:S(2)}) copy-start(s32[2,1024]{1,0:T(2,128)} %emitters.1) | copy-start | bytes 24580
  0.7 0.9 %copy-start.7 = (f32[6]{0:T(128)S(1)}, f32[6]{0:T(128)}, u32[]{:S(2)}) copy-start(f32[6]{0:T(128)} %signature.1) | copy-start | bytes 76
  1.5 0.9 %copy-start = (f32[2,32,512]{2,1,0:T(8,128)S(1)}, f32[2,32,512]{2,1,0:T(8,128)}, u32[]{:S(2)}) copy-start(f32[2,32,512]{2,1,0:T(8,128)} %velocity_in.1) | copy-start | bytes 393220
  2.4 0.9 %copy-start.1 = (bf16[2,2,32,512]{3,2,1,0:T(8,128)(2,1)S(1)}, bf16[2,2,32,512]{3,2,1,0:T(8,128)(2,1)}, u32[]{:S(2)}) copy-start(bf16[2,2,32,512]{3,2,1,0:T(8,128)(2,1)} %preceding_in.1) | copy-start | bytes 393220
  3.3 0.9 %copy-start.2 = (bf16[2,2,32,512]{3,2,1,0:T(8,128)(2,1)S(1)}, bf16[2,2,32,512]{3,2,1,0:T(8,128)(2,1)}, u32[]{:S(2)}) copy-start(bf16[2,2,32,512]{3,2,1,0:T(8,128)(2,1)} %entry_in.1) | copy-start | bytes 393220
  4.2 0.9 %copy-start.3 = (bf16[2,2,32,512]{3,2,1,0:T(8,128)(2,1)S(1)}, bf16[2,2,32,512]{3,2,1,0:T(8,128)(2,1)}, u32[]{:S(2)}) copy-start(bf16[2,2,32,512]{3,2,1,0:T(8,128)(2,1)} %beyond_in.1) | copy-start | bytes 393220
  5.2 0.9 %copy-start.4 = (bf16[2,2,32,512]{3,2,1,0:T(8,128)(2,1)S(1)}, bf16[2,2,32,512]{3,2,1,0:T(8,128)(2,1)}, u32[]{:S(2)}) copy-start(bf16[2,2,32,512]{3,2,1,0:T(8,128)(2,1)} %terminal_in.1) | copy-start | bytes 393220

commit v3 on v2

--- a/solution.py
+++ b/solution.py
@@ -39,10 +39,7 @@
     backward_halo,
     forward_ring,
     backward_ring,
-    preceding_ring,
-    beyond_ring,
-    final_ring,
-    velocity_ring,
+    courant_edge,
     courant,
     courant_ring,
     partial,
@@ -61,14 +58,8 @@
     forward_got,
     backward_sent,
     backward_got,
-    preceding_sent,
-    preceding_got,
-    beyond_sent,
-    beyond_got,
-    final_sent,
-    final_got,
-    velocity_sent,
-    velocity_got,
+    courant_sent,
+    courant_got,
     sums_sent,
     sums_got,
     total_sent,
@@ -140,40 +131,32 @@
             got.at[side, e, s],
         )
 
-    def plane_args(side, field, ring, sent, got, s):
-        edge = last if side == 0 else 0
-        return field.at[s, edge], ring.at[side, s], sent.at[side, s], got.at[side, s]
-
-    def velocity_args(side):
-        edge = last if side == 0 else 0
+    def plane_args(side, field, link, j, s):
+        halo, sent, got = link
+        edge, at = last if side == 0 else 0, j * pairs
         return (
-            velocity_in.at[edge],
-            velocity_ring.at[side],
-            velocity_sent.at[side],
-            velocity_got.at[side],
+            field.at[s, edge],
+            halo.at[side, 0, s, j],
+            sent.at[side, at, s],
+            got.at[side, at, s],
+        )
+
+    def courant_args(side):
+        return (
+            courant_edge.at[side],
+            courant_ring.at[side],
+            courant_sent.at[side],
+            courant_got.at[side],
         )
 
     ahead = [preceding, entry] + [forward.at[j] for j in range(ticks - 1)] + [final]
     back = [beyond, terminal] + [backward.at[j] for j in range(ticks)]
     ahead_link = (forward_halo, forward_sent, forward_got)
     back_link = (backward_halo, backward_sent, backward_got)
-    preceding_link = (preceding_ring, preceding_sent, preceding_got)
-    beyond_link = (beyond_ring, beyond_sent, beyond_got)
-    final_link = (final_ring, final_sent, final_got)
 
     for s in shot_range:
         for side in sides:
-            send(side, *pair_args(side, entry_in, ahead_link, 0, s))
-        for side in sides:
-            send(side, *plane_args(side, preceding_in, *preceding_link, s))
-        if s == 0:
-            for side in sides:
-                send(side, *velocity_args(side))
-    for s in shot_range:
-        for side in sides:
-            send(side, *pair_args(side, terminal_in, back_link, 0, s))
-        for side in sides:
-            send(side, *plane_args(side, beyond_in, *beyond_link, s))
+            send(side, *plane_args(side, entry_in, ahead_link, 0, s))
 
     for side, here in ((0, me == 0), (1, me == peers - 1)):
 
@@ -182,10 +165,7 @@
             for ring in (
                 forward_halo,
                 backward_halo,
-                preceding_ring,
-                beyond_ring,
-                final_ring,
-                velocity_ring,
+                courant_ring,
             ):
                 ring[side] = jnp.zeros_like(ring[side])
 
@@ -243,13 +223,26 @@
     def near(halo, side, e, s):
         return halo[side, e, s, 1 - side]
 
-    def begin(fields, e, s, source):
-        for z in plane_range:
-            partial[s, z] = inner(fields[2 * e], fields[2 * e + 1], s, z) + source(
-                2 * e, s, z + 1, fields
-            )
-
-    def two_steps(fields, link, rings, e, s, before, source, ring_source):
+    def begin(fields, j, s, source):
+        for z in plane_range:
+            partial[s, z] = inner(fields[j], fields[j + 1], s, z) + source(j, s, z + 1)
+
+    def one_step(fields, link, j, s):
+        halo, following = link[0], fields[j + 2]
+        for z in plane_range:
+            value = partial[s, z]
+            if z == 0:
+                value += courant[z] * halo[0, 0, s, j].astype(F32)
+            if z == last:
+                value += courant[z] * halo[1, 0, s, j].astype(F32)
+            following[s, z] = value.astype(BF16)
+        for side in sides:
+            if j == 0:
+                send(side, *plane_args(side, following, link, 1, s))
+            else:
+                send(side, *pair_args(side, following, link, 1, s))
+
+    def two_steps(fields, link, rings, e, s, source, ring_source):
         halo = link[0]
         j = 2 * e
         earlier, current, middle, after = fields[j : j + 4]
@@ -264,11 +257,12 @@
             x = near(halo, side, e, s).astype(F32)
             around = in_plane(x) + halo[side, e, s, side].astype(F32)
             around += current[s, 0 if side == 0 else last].astype(F32)
-            old = before[side, s] if e == 0 else rings[side, e - 1, s]
-            value = 2.0 * x - old.astype(F32) + courant_ring[side] * (around - 6.0 * x)
+            old = halo[side, 0, s, 1] if e == 1 else rings[side, e - 1, s]
+            value = 2.0 * x - old.astype(F32)
+            value += courant_ring[side].astype(F32) * (around - 6.0 * x)
             rings[side, e, s] = (value + ring_source(e, s, side)).astype(BF16)
         for z in plane_range:
-            value = inner(current, middle, s, z) + source(j + 1, s, z + 1, fields)
+            value = inner(current, middle, s, z) + source(j + 1, s, z + 1)
             if z == 0:
                 value += courant[z] * rings[0, e, s].astype(F32)
             if z == last:
@@ -278,7 +272,7 @@
             for side in sides:
                 send(side, *pair_args(side, after, link, e + 1, s))
 
-    def fire(j, s, w, fields):
+    def fire(j, s, w):
         return signature[j] * fired[s, w]
 
     def fire_ring(e, s, side):
@@ -299,29 +293,42 @@
     for load in loads:
         load.wait()
     courant[...] = (velocity[...] * SPEED_SCALE) ** 2
+    courant_edge[0] = courant[last].astype(BF16)
+    courant_edge[1] = courant[0].astype(BF16)
     for s in shot_range:
         begin(ahead, 0, s, fire)
-    for k in range(ticks):
-        record(k)
+
+    for j in (0, 1):
+        for s in shot_range:
+            for side in sides:
+                receive(side, *plane_args(side, ahead[j + 1], ahead_link, j, s))
+            one_step(ahead, ahead_link, j, s)
+            begin(ahead, j + 1, s, fire)
+        if j == 0:
+            for side in sides:
+                send(side, *courant_args(side))
+        record(2 * j)
+        record(2 * j + 1)
+    for s in shot_range:
+        correlate(0, s)
+        correlate(1, s)
     for side in sides:
-        receive(side, *velocity_args(side))
-    courant_ring[...] = (velocity_ring[...] * SPEED_SCALE) ** 2
-
-    for e in range(pairs):
+        receive(side, *courant_args(side))
+
+    for e in range(1, pairs):
         for s in shot_range:
             for side in sides:
                 receive(side, *pair_args(side, ahead[2 * e + 1], ahead_link, e, s))
-            if e == 0:
+            two_steps(ahead, ahead_link, forward_ring, e, s, fire, fire_ring)
+            if e < pairs - 1:
+                begin(ahead, 2 * e + 2, s, fire)
+        if e == 1:
+            for s in shot_range:
                 for side in sides:
-                    receive(side, *plane_args(side, preceding_in, *preceding_link, s))
-            two_steps(
-                ahead, ahead_link, forward_ring, e, s, preceding_ring, fire, fire_ring
-            )
-            if e < pairs - 1:
-                begin(ahead, e + 1, s, fire)
-            else:
-                for side in sides:
-                    send(side, *plane_args(side, final, *final_link, s))
+                    send(side, *plane_args(side, terminal_in, back_link, 0, s))
+            for k in range(4, ticks):
+                record(k)
+        for s in shot_range:
             correlate(2 * e, s)
             correlate(2 * e + 1, s)
 
@@ -358,11 +365,9 @@
     gathered[me] = block
 
     for s in shot_range:
-        begin(back, 0, s, lambda j, s, w, fields: -recorded[ticks - 1, s, w])
+        begin(back, 0, s, lambda j, s, w: -recorded[ticks - 1, s, w])
         for side in sides:
-            receive(side, *pair_args(side, terminal_in, back_link, 0, s))
-            receive(side, *plane_args(side, beyond_in, *beyond_link, s))
-            receive(side, *plane_args(side, final, *final_link, s))
+            receive(side, *plane_args(side, terminal_in, back_link, 0, s))
 
     for d in range(1, peers):
         shared(d).wait_recv()
@@ -380,14 +385,14 @@
             p = final[s, z].astype(F32)
             partial[s, z] = partial[s, z] + scales[s] * (tally[z + 1] * p)
 
-    def residue(j, s, w, fields):
+    def residue(j, s, w):
         k = ticks - 1 - j
         p = ahead[k + 2][s, w - 1].astype(F32)
         return scales[s] * (tally[w] * p) - recorded[k, s, w]
 
     def residue_ring(e, s, side):
         w = 0 if side == 0 else wide - 1
-        p = final_ring[side, s] if e == 0 else near(forward_halo, side, pairs - e, s)
+        p = near(forward_halo, side, pairs - e, s)
         return scales[s] * (tally[w] * p.astype(F32)) - recorded[ticks - 1 - 2 * e, s, w]
 
     def gather_total(j, z):
@@ -412,16 +417,23 @@
             device_id_type=MESH,
         )
 
-    for e in range(pairs):
-        for s in shot_range:
-            if e:
+    for j in (0, 1):
+        for s in shot_range:
+            if j:
                 for side in sides:
-                    receive(side, *pair_args(side, back[2 * e + 1], back_link, e, s))
-            two_steps(
-                back, back_link, backward_ring, e, s, beyond_ring, residue, residue_ring
-            )
+                    receive(side, *plane_args(side, back[j + 1], back_link, j, s))
+            one_step(back, back_link, j, s)
+            begin(back, j + 1, s, residue)
+        for z in plane_range:
+            total[z] = gather_total(j, z)
+
+    for e in range(1, pairs):
+        for s in shot_range:
+            for side in sides:
+                receive(side, *pair_args(side, back[2 * e + 1], back_link, e, s))
+            two_steps(back, back_link, backward_ring, e, s, residue, residue_ring)
             if e < pairs - 1:
-                begin(back, e + 1, s, residue)
+                begin(back, 2 * e + 2, s, residue)
         for z in plane_range:
             total[z] = gather_total(2 * e, z)
             value = gather_total(2 * e + 1, z)
@@ -480,12 +492,9 @@
             pltpu.VMEM((2, pairs, shots, 2, rows, cols), BF16),
             pltpu.VMEM((2, pairs, shots, rows, cols), BF16),
             pltpu.VMEM((2, pairs, shots, rows, cols), BF16),
-            pltpu.VMEM((2, shots, rows, cols), BF16),
-            pltpu.VMEM((2, shots, rows, cols), BF16),
-            pltpu.VMEM((2, shots, rows, cols), BF16),
-            pltpu.VMEM((2, rows, cols), F32),
+            pltpu.VMEM((2, rows, cols), BF16),
             pltpu.VMEM(slab, F32),
-            pltpu.VMEM((2, rows, cols), F32),
+            pltpu.VMEM((2, rows, cols), BF16),
             pltpu.VMEM((shots,) + slab, F32),
             pltpu.VMEM((cols, probes), BF16),
             pltpu.VMEM(wide, F32),
@@ -498,16 +507,10 @@
             pltpu.VMEM(slab, BF16),
             pltpu.VMEM(slab, BF16),
             dma((5,)),
-            dma((2, pairs, shots)),
-            dma((2, pairs, shots)),
-            dma((2, pairs, shots)),
-            dma((2, pairs, shots)),
-            dma((2, shots)),
-            dma((2, shots)),
-            dma((2, shots)),
-            dma((2, shots)),
-            dma((2, shots)),
-            dma((2, shots)),
+            dma((2, pairs + 1, shots)),
+            dma((2, pairs + 1, shots)),
+            dma((2, pairs + 1, shots)),
+            dma((2, pairs + 1, shots)),
             dma((2,)),
             dma((2,)),
             dma((peers,)),

time: 69.8 us -> 61 us (0.87)
  Pallas kernels: 61.7 us -> 52.9 us
    pallas_call x1, Pallas kernels: 61.7 us -> 52.9 us  [body(): pl.pallas_call(functools.partial(kernel, peers), out_shape=(jax.ShapeDtyp...]
where the time goes in v3:
time: 61 us; the launch traced here: 60.8 us
  Pallas kernels  52.9 us (87%)
  local copies, waits for them, and re-layouts  7.19 us (12%)
  between operations  0.7 us (1%)
    pallas_call x1, Pallas kernels, body(): pl.pallas_call(functools.partial(kernel, peers), out_shape=(jax.ShapeDtyp...  52.9 us
    unnamed x20, local copies, waits for them, and re-layouts  7.19 us

profile of v3, /device:TPU:0, one launch (start us, length us, event | category | flops | bytes accessed | tf_op | source)
XLA Modules:
  0.0 60.8 jit_solution(16980445988970286431)
XLA Ops:
  0.6 0.0 copy-start.5
  0.6 0.0 copy-start.6
  0.7 0.0 copy-start.7
  0.7 0.8 %copy.12.recordings = f32[2,6,1024]{2,1,0:T(8,128)S(1)} copy(f32[2,6,1024]{2,0,1:T(2,128)} %param.17) | data formatting | bytes 98304 | tf_op args[8]
  1.5 0.0 copy-done.5
  1.5 0.0 copy-done.6
  1.5 0.0 copy-done.7
  1.5 0.0 copy-start
  1.5 0.9 %copy-done = f32[2,32,512]{2,1,0:T(8,128)S(1)} copy-done((f32[2,32,512]{2,1,0:T(8,128)S(1)}, f32[2,32,512]{2,1,0:T(8,128)}, u32[]{:S(2)}) %copy-start) | copy-done | bytes 131096
  2.4 0.0 copy-start.1
  2.4 0.9 %copy-done.1 = bf16[2,2,32,512]{3,2,1,0:T(8,128)(2,1)S(1)} copy-done((bf16[2,2,32,512]{3,2,1,0:T(8,128)(2,1)S(1)}, bf16[2,2,32,512]{3,2,1,0:T(8,128)(2,1)}, u32[]{:S(2)}) %copy-start.1) | copy-done | bytes 131096
  3.3 0.0 copy-start.2
  3.3 0.9 %copy-done.2 = bf16[2,2,32,512]{3,2,1,0:T(8,128)(2,1)S(1)} copy-done((bf16[2,2,32,512]{3,2,1,0:T(8,128)(2,1)S(1)}, bf16[2,2,32,512]{3,2,1,0:T(8,128)(2,1)}, u32[]{:S(2)}) %copy-start.2) | copy-done | bytes 131096
  4.2 0.0 copy-start.3
  4.2 0.9 %copy-done.3 = bf16[2,2,32,512]{3,2,1,0:T(8,128)(2,1)S(1)} copy-done((bf16[2,2,32,512]{3,2,1,0:T(8,128)(2,1)S(1)}, bf16[2,2,32,512]{3,2,1,0:T(8,128)(2,1)}, u32[]{:S(2)}) %copy-start.3) | copy-done | bytes 131096
  5.2 0.0 copy-start.4
  5.2 0.9 %copy-done.4 = bf16[2,2,32,512]{3,2,1,0:T(8,128)(2,1)S(1)} copy-done((bf16[2,2,32,512]{3,2,1,0:T(8,128)(2,1)S(1)}, bf16[2,2,32,512]{3,2,1,0:T(8,128)(2,1)}, u32[]{:S(2)}) %copy-start.4) | copy-done | bytes 131096
  6.1 52.9 %shard_map.112 = (bf16[2,2,32,512]{3,2,1,0:T(8,128)(2,1)S(1)}, f32[2]{0:T(128)S(1)}, f32[2,32,512]{2,1,0:T(8,128)S(1)}) custom-call(f32[2,32,512]{2,1,0:T(8,128)S(1)} %copy-done, bf16[2,2,32,512]{3,2,1,0:T(8,128)(2,1)S(1)} %copy-done.1, bf16[2,2,32,512]{3,2,1,0:T(8,128)(2,1)S(1)} %copy-done.2, bf16[2,2,32,512]{3,2,1,0:T(8,128)(2,1)S(1)} %copy-done.3, ...), custom_call_target="tpu_custom_call" | custom-call | tf_op jit(solution)/shard_map/pallas_call | solution.py:474
  58.9 0.7 %copy.16 = bf16[2,2,32,512]{3,2,1,0:T(8,128)(2,1)} copy(bf16[2,2,32,512]{3,2,1,0:T(8,128)(2,1)S(1)} %get-tuple-element.6) | data formatting | bytes 262144
  59.6 0.5 copy.17
  60.1 0.7 %copy.18 = f32[2,32,512]{2,1,0:T(8,128)} copy(f32[2,32,512]{2,1,0:T(8,128)S(1)} %get-tuple-element.8) | data formatting | bytes 262144
Async XLA Ops:
  0.6 0.9 %copy-start.5 = (s32[3,1024]{1,0:T(4,128)S(1)}, s32[3,1024]{1,0:T(4,128)}, u32[]{:S(2)}) copy-start(s32[3,1024]{1,0:T(4,128)} %locations.1) | copy-start | bytes 36868
  0.6 0.9 %copy-start.6 = (s32[2,1024]{1,0:T(2,128)S(1)}, s32[2,1024]{1,0:T(2,128)}, u32[]{:S(2)}) copy-start(s32[2,1024]{1,0:T(2,128)} %emitters.1) | copy-start | bytes 24580
  0.7 0.9 %copy-start.7 = (f32[6]{0:T(128)S(1)}, f32[6]{0:T(128)}, u32[]{:S(2)}) copy-start(f32[6]{0:T(128)} %signature.1) | copy-start | bytes 76
  1.5 0.9 %copy-start = (f32[2,32,512]{2,1,0:T(8,128)S(1)}, f32[2,32,512]{2,1,0:T(8,128)}, u32[]{:S(2)}) copy-start(f32[2,32,512]{2,1,0:T(8,128)} %velocity_in.1) | copy-start | bytes 393220
  2.4 0.9 %copy-start.1 = (bf16[2,2,32,512]{3,2,1,0:T(8,128)(2,1)S(1)}, bf16[2,2,32,512]{3,2,1,0:T(8,128)(2,1)}, u32[]{:S(2)}) copy-start(bf16[2,2,32,512]{3,2,1,0:T(8,128)(2,1)} %preceding_in.1) | copy-start | bytes 393220
  3.3 0.9 %copy-start.2 = (bf16[2,2,32,512]{3,2,1,0:T(8,128)(2,1)S(1)}, bf16[2,2,32,512]{3,2,1,0:T(8,128)(2,1)}, u32[]{:S(2)}) copy-start(bf16[2,2,32,512]{3,2,1,0:T(8,128)(2,1)} %entry_in.1) | copy-start | bytes 393220
  4.2 0.9 %copy-start.3 = (bf16[2,2,32,512]{3,2,1,0:T(8,128)(2,1)S(1)}, bf16[2,2,32,512]{3,2,1,0:T(8,128)(2,1)}, u32[]{:S(2)}) copy-start(bf16[2,2,32,512]{3,2,1,0:T(8,128)(2,1)} %beyond_in.1) | copy-start | bytes 393220
  5.2 0.9 %copy-start.4 = (bf16[2,2,32,512]{3,2,1,0:T(8,128)(2,1)S(1)}, bf16[2,2,32,512]{3,2,1,0:T(8,128)(2,1)}, u32[]{:S(2)}) copy-start(bf16[2,2,32,512]{3,2,1,0:T(8,128)(2,1)} %terminal_in.1) | copy-start | bytes 393220

commit v4 on v3

--- a/solution.py
+++ b/solution.py
@@ -191,15 +191,11 @@
     fired[...] = placed[cells:].reshape(shots, wide, rows, cols)
 
     def record(k):
-        for s in shot_range:
-            row = recordings[s, k : k + 1, :]
-            high = row.astype(BF16).astype(F32)
-            lefts = [
-                jnp.where(row_hot, high, 0.0).astype(BF16),
-                jnp.where(row_hot, row - high, 0.0).astype(BF16),
-            ]
-            both = spread(jnp.concatenate(lefts, axis=0)).reshape(2, wide, rows, cols)
-            recorded[k, s] = both[0] + both[1]
+        lefts = [
+            jnp.where(row_hot, recordings[s, k : k + 1, :], 0.0).astype(BF16) for s in shot_range
+        ]
+        both = spread(jnp.concatenate(lefts, axis=0))
+        recorded[k] = both.reshape(shots, wide, rows, cols)
 
     row_at = lax.broadcasted_iota(jnp.int32, (rows, cols), 0)
     col_at = lax.broadcasted_iota(jnp.int32, (rows, cols), 1)

time: 61 us -> 61 us (level)
  no operation moved by 1% of the time
where the time goes in v4:
time: 61 us; the launch traced here: 60.8 us
  Pallas kernels  52.9 us (87%)
  local copies, waits for them, and re-layouts  7.19 us (12%)
  between operations  0.7 us (1%)
    pallas_call x1, Pallas kernels, body(): pl.pallas_call(functools.partial(kernel, peers), out_shape=(jax.ShapeDtyp...  52.9 us
    unnamed x20, local copies, waits for them, and re-layouts  7.19 us

profile of v4, /device:TPU:0, one launch (start us, length us, event | category | flops | bytes accessed | tf_op | source)
XLA Modules:
  0.0 60.8 jit_solution(12072155583806870546)
XLA Ops:
  0.6 0.0 copy-start.5
  0.6 0.0 copy-start.6
  0.7 0.0 copy-start.7
  0.7 0.8 %copy.12.recordings = f32[2,6,1024]{2,1,0:T(8,128)S(1)} copy(f32[2,6,1024]{2,0,1:T(2,128)} %param.17) | data formatting | bytes 98304 | tf_op args[8]
  1.5 0.0 copy-done.5
  1.5 0.0 copy-done.6
  1.5 0.0 copy-done.7
  1.5 0.0 copy-start
  1.5 0.9 %copy-done = f32[2,32,512]{2,1,0:T(8,128)S(1)} copy-done((f32[2,32,512]{2,1,0:T(8,128)S(1)}, f32[2,32,512]{2,1,0:T(8,128)}, u32[]{:S(2)}) %copy-start) | copy-done | bytes 131096
  2.4 0.0 copy-start.1
  2.4 0.9 %copy-done.1 = bf16[2,2,32,512]{3,2,1,0:T(8,128)(2,1)S(1)} copy-done((bf16[2,2,32,512]{3,2,1,0:T(8,128)(2,1)S(1)}, bf16[2,2,32,512]{3,2,1,0:T(8,128)(2,1)}, u32[]{:S(2)}) %copy-start.1) | copy-done | bytes 131096
  3.3 0.0 copy-start.2
  3.3 0.9 %copy-done.2 = bf16[2,2,32,512]{3,2,1,0:T(8,128)(2,1)S(1)} copy-done((bf16[2,2,32,512]{3,2,1,0:T(8,128)(2,1)S(1)}, bf16[2,2,32,512]{3,2,1,0:T(8,128)(2,1)}, u32[]{:S(2)}) %copy-start.2) | copy-done | bytes 131096
  4.2 0.0 copy-start.3
  4.2 0.9 %copy-done.3 = bf16[2,2,32,512]{3,2,1,0:T(8,128)(2,1)S(1)} copy-done((bf16[2,2,32,512]{3,2,1,0:T(8,128)(2,1)S(1)}, bf16[2,2,32,512]{3,2,1,0:T(8,128)(2,1)}, u32[]{:S(2)}) %copy-start.3) | copy-done | bytes 131096
  5.2 0.0 copy-start.4
  5.2 0.9 %copy-done.4 = bf16[2,2,32,512]{3,2,1,0:T(8,128)(2,1)S(1)} copy-done((bf16[2,2,32,512]{3,2,1,0:T(8,128)(2,1)S(1)}, bf16[2,2,32,512]{3,2,1,0:T(8,128)(2,1)}, u32[]{:S(2)}) %copy-start.4) | copy-done | bytes 131096
  6.1 52.9 %shard_map.112 = (bf16[2,2,32,512]{3,2,1,0:T(8,128)(2,1)S(1)}, f32[2]{0:T(128)S(1)}, f32[2,32,512]{2,1,0:T(8,128)S(1)}) custom-call(f32[2,32,512]{2,1,0:T(8,128)S(1)} %copy-done, bf16[2,2,32,512]{3,2,1,0:T(8,128)(2,1)S(1)} %copy-done.1, bf16[2,2,32,512]{3,2,1,0:T(8,128)(2,1)S(1)} %copy-done.2, bf16[2,2,32,512]{3,2,1,0:T(8,128)(2,1)S(1)} %copy-done.3, ...), custom_call_target="tpu_custom_call" | custom-call | tf_op jit(solution)/shard_map/pallas_call | solution.py:470
  58.9 0.7 %copy.16 = bf16[2,2,32,512]{3,2,1,0:T(8,128)(2,1)} copy(bf16[2,2,32,512]{3,2,1,0:T(8,128)(2,1)S(1)} %get-tuple-element.6) | data formatting | bytes 262144
  59.6 0.5 copy.17
  60.1 0.7 %copy.18 = f32[2,32,512]{2,1,0:T(8,128)} copy(f32[2,32,512]{2,1,0:T(8,128)S(1)} %get-tuple-element.8) | data formatting | bytes 262144
Async XLA Ops:
  0.6 0.9 %copy-start.5 = (s32[3,1024]{1,0:T(4,128)S(1)}, s32[3,1024]{1,0:T(4,128)}, u32[]{:S(2)}) copy-start(s32[3,1024]{1,0:T(4,128)} %locations.1) | copy-start | bytes 36868
  0.6 0.9 %copy-start.6 = (s32[2,1024]{1,0:T(2,128)S(1)}, s32[2,1024]{1,0:T(2,128)}, u32[]{:S(2)}) copy-start(s32[2,1024]{1,0:T(2,128)} %emitters.1) | copy-start | bytes 24580
  0.7 0.9 %copy-start.7 = (f32[6]{0:T(128)S(1)}, f32[6]{0:T(128)}, u32[]{:S(2)}) copy-start(f32[6]{0:T(128)} %signature.1) | copy-start | bytes 76
  1.5 0.9 %copy-start = (f32[2,32,512]{2,1,0:T(8,128)S(1)}, f32[2,32,512]{2,1,0:T(8,128)}, u32[]{:S(2)}) copy-start(f32[2,32,512]{2,1,0:T(8,128)} %velocity_in.1) | copy-start | bytes 393220
  2.4 0.9 %copy-start.1 = (bf16[2,2,32,512]{3,2,1,0:T(8,128)(2,1)S(1)}, bf16[2,2,32,512]{3,2,1,0:T(8,128)(2,1)}, u32[]{:S(2)}) copy-start(bf16[2,2,32,512]{3,2,1,0:T(8,128)(2,1)} %preceding_in.1) | copy-start | bytes 393220
  3.3 0.9 %copy-start.2 = (bf16[2,2,32,512]{3,2,1,0:T(8,128)(2,1)S(1)}, bf16[2,2,32,512]{3,2,1,0:T(8,128)(2,1)}, u32[]{:S(2)}) copy-start(bf16[2,2,32,512]{3,2,1,0:T(8,128)(2,1)} %entry_in.1) | copy-start | bytes 393220
  4.2 0.9 %copy-start.3 = (bf16[2,2,32,512]{3,2,1,0:T(8,128)(2,1)S(1)}, bf16[2,2,32,512]{3,2,1,0:T(8,128)(2,1)}, u32[]{:S(2)}) copy-start(bf16[2,2,32,512]{3,2,1,0:T(8,128)(2,1)} %beyond_in.1) | copy-start | bytes 393220
  5.2 0.9 %copy-start.4 = (bf16[2,2,32,512]{3,2,1,0:T(8,128)(2,1)S(1)}, bf16[2,2,32,512]{3,2,1,0:T(8,128)(2,1)}, u32[]{:S(2)}) copy-start(bf16[2,2,32,512]{3,2,1,0:T(8,128)(2,1)} %terminal_in.1) | copy-start | bytes 393220
